TPU v7x, 128 devices: a whole 4x4x4 slice. The times are simulated.
128 devices in a mesh: gauss: 4 (over x), pix: 32 (over y, z, core).
Axes of the slice: x: 4, y: 4, z: 4, core: 2. Of those that a mesh axis runs over, the one named last changes fastest.
Arguments:
- params: float32 [54, 2097152], P(None, ('gauss', 'pix')), may hold values from -8 to 22, as said below
- angles_next: float32 [2048, 2], P(('gauss', 'pix')), may hold values from -3.140625 to 3.140625
- angles_cur: float32 [2048, 2], P(('gauss', 'pix')), may hold values from -3.140625 to 3.140625
- lists_next: int32 [2048, 256], P(('gauss', 'pix')), may hold values from 0 to 4095, as said below
- lists_cur: int32 [2048, 256], P(('gauss', 'pix')), may hold values from 0 to 4095, as said below
- counts_next: int32 [2048], P(('gauss', 'pix')), may hold values from 97 to 256, as said below
- counts_cur: int32 [2048], P(('gauss', 'pix')), may hold values from 97 to 256, as said below
- sends_next: int32 [128, 128, 32], P(('gauss', 'pix')), may hold values from 0 to 16383
- sends_cur: int32 [128, 128, 32], P(('gauss', 'pix')), may hold values from 0 to 16383
- cotangent: float32 [2048, 3, 256], P(('gauss', 'pix')), may hold values from -6 to 6
Outputs:
- image_next: float32 [2048, 3, 256], P(('gauss', 'pix'))
- grads: float32 [54, 2097152], P(None, ('gauss', 'pix'))
Inputs may be any that keep to these rules, and one draw needn't show every extreme that they name: `params`: gaussian parameters: rows 2 and 4 (conic diagonal) lie in 0.01 to 0.1, row 3 below 0.8 sqrt(row 2 * row 4) in magnitude, row 5 in -8 to 5. `lists_next`: within the 16 tiles of one device, every slot of that device appears exactly once among all entries, live or padding. `lists_cur`: within the 16 tiles of one device, every slot of that device appears exactly once among all entries, live or padding. `counts_next`: live entries at the front of each tile's list; the rest is padding. `counts_cur`: live entries at the front of each tile's list; the rest is padding.
All inputs are finite; a program needn't handle non-finite values.
Results may differ from a plain program's by a relative error of at most 0.0003.
Values sent between devices are 32-bit elements; how exact they have to be, the bound alone decides.
A program may use at most 128 MiB of HBM per device.

v0:
```python
import jax
import jax.numpy as jnp
import numpy as np
from jax import lax
from jax.experimental import pallas as pl
from jax.experimental.pallas import tpu as pltpu
from jax.sharding import PartitionSpec as P

F32 = jnp.float32
BF16 = jnp.bfloat16
I32 = jnp.int32
AXES = ("gauss", "pix")
N_DEV = 128
N_PIX = 32
SLOTS = 32
GAUSS = 16384
HALF = 8192
ROWS = 54
LANES = 128
STEPS = 32
LOG2E = 1.4426950408889634
VMEM_LIMIT = 56 * 2**20


def iota(shape, dim):
    return lax.broadcasted_iota(I32, shape, dim)


def dot_nn(a, b):
    return lax.dot_general(a, b, (((1,), (0,)), ((), ())), preferred_element_type=F32)


def dot_nt(a, b):
    return lax.dot_general(a, b, (((1,), (1,)), ((), ())), preferred_element_type=F32)


def split2(x):
    high = x.astype(BF16)
    low = (x - high.astype(F32)).astype(BF16)
    return high, low


def split3(x):
    high = x.astype(BF16)
    rest = x - high.astype(F32)
    mid = rest.astype(BF16)
    low = (rest - mid.astype(F32)).astype(BF16)
    return high, mid, low


def pixel_tables():
    pixels = np.arange(256)
    qx = (pixels % 16) - 7.5
    qy = (pixels // 16) - 7.5
    mono = np.stack([np.ones(256), qx, qy, qx * qx, qx * qy, qy * qy], 0)
    power = np.zeros((32, 640), np.float32)
    for part in range(3):
        power[part * 6 : part * 6 + 6, :256] = mono
        for ch in range(3):
            power[18 + part * 3 + ch, 256 + 128 * ch : 384 + 128 * ch] = 1.0
    moments = np.zeros((16, 512), np.float32)
    moments[:6, :256] = mono
    moments[:6, 256:] = mono
    return jnp.asarray(power, BF16), jnp.asarray(moments, BF16)


def order_lists(lists_ref, turned, slots_ref):
    turned[:, 0:16] = lists_ref[...].astype(F32).T
    lane_group = iota((STEPS, LANES), 1) // 16
    out = jnp.zeros((STEPS, LANES), F32)
    for k in range(8):
        piece = pltpu.roll(turned[pl.ds(k, STEPS, stride=8), :], 16 * k, 1) if k else turned[pl.ds(0, STEPS, stride=8), :]
        out = jnp.where(lane_group == k, piece, out)
    slots_ref[...] = out.astype(I32)


def owner_onehot(slots_ref, hot_ref):
    rows = iota((N_DEV, LANES), 0)
    for q in range(STEPS):
        owner = slots_ref[q : q + 1, :] // SLOTS
        hot_ref[:, q * LANES : (q + 1) * LANES] = (rows == owner).astype(F32).astype(BF16)


def slot_tiles(slots_ref, hot_ref, mark_ref):
    rows = iota((SLOTS, LANES), 0)
    tile = (iota((SLOTS, LANES), 1) % 16).astype(F32)
    for q in range(STEPS):
        place = slots_ref[q : q + 1, :] % SLOTS
        mark_ref[:, q * LANES : (q + 1) * LANES] = jnp.where(rows == place, tile, 0.0).astype(BF16)
    return dot_nt(hot_ref[...], mark_ref[...])


def angle_message(tiles_next, tiles_cur, angles_next, angles_cur):
    tiles = jnp.concatenate([tiles_next, tiles_next, tiles_cur, tiles_cur], 1)
    region = iota((1, LANES), 1) // 32
    out = jnp.zeros((N_DEV, LANES), F32)
    for t in range(16):
        row = jnp.where(
            region < 2,
            jnp.where(region == 0, angles_next[t, 0], angles_next[t, 1]),
            jnp.where(region == 2, angles_cur[t, 0], angles_cur[t, 1]),
        )
        out = jnp.where(tiles == float(t), row, out)
    return out


def lists_kernel(lists_next, lists_cur, angles_next, angles_cur, msg, slots_next, slots_cur, hot_next, hot_cur, turned, mark):
    order_lists(lists_next, turned, slots_next)
    owner_onehot(slots_next, hot_next)
    tiles_next = slot_tiles(slots_next, hot_next, mark)
    order_lists(lists_cur, turned, slots_cur)
    owner_onehot(slots_cur, hot_cur)
    tiles_cur = slot_tiles(slots_cur, hot_cur, mark)
    msg[:, 0, :] = angle_message(tiles_next, tiles_cur, angles_next, angles_cur)


def sh_terms(theta, azimuth):
    sin_t = jnp.sin(theta)
    dir_x = sin_t * jnp.cos(azimuth)
    dir_y = sin_t * jnp.sin(azimuth)
    dir_z = jnp.cos(theta)
    sq_x = dir_x * dir_x
    sq_y = dir_y * dir_y
    sq_z = dir_z * dir_z
    return [
        0.28209479177387814 * jnp.ones_like(dir_x),
        -0.4886025119029199 * dir_y,
        0.4886025119029199 * dir_z,
        -0.4886025119029199 * dir_x,
        1.0925484305920792 * dir_x * dir_y,
        -1.0925484305920792 * dir_y * dir_z,
        0.31539156525252005 * (2.0 * sq_z - sq_x - sq_y),
        -1.0925484305920792 * dir_x * dir_z,
        0.5462742152960396 * (sq_x - sq_y),
        -0.5900435899266435 * dir_y * (3.0 * sq_x - sq_y),
        2.890611442640554 * dir_x * dir_y * dir_z,
        -0.4570457994644658 * dir_y * (4.0 * sq_z - sq_x - sq_y),
        0.3731763325901154 * dir_z * (2.0 * sq_z - 3.0 * sq_x - 3.0 * sq_y),
        -0.4570457994644658 * dir_x * (4.0 * sq_z - sq_x - sq_y),
        1.445305721320277 * dir_z * (sq_x - sq_y),
        -0.5900435899266435 * dir_x * (sq_x - 3.0 * sq_y),
    ]


def build_table(params, table):
    zeros = jnp.zeros((64 - ROWS, LANES), F32)

    def block(b, _):
        first = pl.multiple_of(b * LANES, LANES)
        both = jnp.concatenate(
            [params[:, pl.ds(first, LANES)], zeros, params[:, pl.ds(first + HALF, LANES)], zeros], 0
        )
        table[pl.ds(first, LANES), :] = both.T
        return 0

    lax.fori_loop(0, HALF // LANES, block, 0, unroll=4)


def gather_rows(index, table, rows, half_ref, turned):
    def pair(r2, _):
        for u in range(256):
            rows[u : u + 1, :] = table[pl.ds(index[r2 * 2 + u // 128, u % 128], 1), :]
        for k in range(2):
            r = r2 * 2 + k
            both = rows[k * 128 : k * 128 + 128, :].T
            upper = half_ref[pl.ds(r, 1), :] > 0.5
            turned[pl.ds(pl.multiple_of(r * 64, 64), 64), :] = jnp.where(upper, both[64:], both[:64])
        return 0

    lax.fori_loop(0, SLOTS // 2, pair, 0)


def split_index(sends_ref, row_ref, half_ref):
    turned = sends_ref[...].astype(F32).T
    upper = turned >= float(HALF)
    half_ref[...] = upper.astype(F32)
    row_ref[...] = jnp.where(upper, turned - float(HALF), turned).astype(I32)


def color_rows(basis, turned, color):
    def one(r, _):
        terms = basis[pl.ds(r, 16, stride=32), :]
        for ch in range(3):
            start = r * 64 + 6 + 16 * ch
            color[pl.ds(ch * 32 + r, 1), :] = 0.5 + jnp.sum(terms * turned[pl.ds(start, 16), :], axis=0, keepdims=True)
        return 0

    lax.fori_loop(0, SLOTS, one, 0, unroll=4)


def owner_message(turned, color, msg):
    geo = [turned[pl.ds(v, 32, stride=64), :] for v in range(6)]
    msg[:, 0, 0:128] = jnp.concatenate(geo[0:4], 0).T
    msg[:, 0, 128:256] = jnp.concatenate([geo[4], geo[5], color[0:32], color[32:64]], 0).T
    last = color[64:96]
    msg[:, 0, 256:384] = jnp.concatenate([last, last, last, last], 0).T


def owner_kernel(
    params, sends_next, sends_cur, angles, msg_next, msg_cur, basis_cur,
    table, rows, turned, row_v, half_next, half_cur, row_next, row_cur, basis_next, color, sem,
):
    split_index(sends_next, row_v, half_next)
    copy = pltpu.make_async_copy(row_v, row_next, sem)
    copy.start()
    copy.wait()
    split_index(sends_cur, row_v, half_cur)
    copy = pltpu.make_async_copy(row_v, row_cur, sem)
    copy.start()
    copy.wait()
    build_table(params, table)
    seen = angles[:, 0, :].T
    for k, term in enumerate(sh_terms(seen[0:32], seen[32:64])):
        basis_next[k * 32 : k * 32 + 32, :] = term
    for k, term in enumerate(sh_terms(seen[64:96], seen[96:128])):
        basis_cur[k * 32 : k * 32 + 32, :] = term
    gather_rows(row_cur, table, rows, half_cur, turned)
    color_rows(basis_cur, turned, color)
    owner_message(turned, color, msg_cur)
    gather_rows(row_next, table, rows, half_next, turned)
    color_rows(basis_next, turned, color)
    owner_message(turned, color, msg_next)


def entries_in_order(got, hot, slots, split, entry):
    for g, size in ((0, 128), (1, 128), (2, 32)):
        parts = split3(got[:, 0, g * 128 : g * 128 + 128].T[0:size])
        for k in range(3):
            split[g * 128 : g * 128 + size, k * 128 : k * 128 + 128] = parts[k]
    rows = iota((SLOTS, LANES), 0)

    def step(q, _):
        cols = hot[:, pl.ds(pl.multiple_of(q * LANES, LANES), LANES)]
        picked = dot_nn(split[...], jnp.concatenate([cols, cols, cols], 0))
        here = rows == slots[pl.ds(q, 1), :] % SLOTS
        for v in range(9):
            kept = jnp.where(here, picked[v * 32 : v * 32 + 32], 0.0)
            entry[pl.ds(v * 32 + q, 1), :] = jnp.sum(kept, axis=0, keepdims=True)
        return 0

    lax.fori_loop(0, STEPS, step, 0, unroll=2)


def power_factors(entry, counts, factor):
    x = entry[0:32] - 8.0
    y = entry[32:64] - 8.0
    con_a = entry[64:96]
    con_b = entry[96:128]
    con_c = entry[128:160]
    logit = entry[160:192]
    position = iota((STEPS, LANES), 0) * 8 + iota((STEPS, LANES), 1) // 16
    tile = iota((STEPS, LANES), 1) % 16
    count = jnp.zeros((STEPS, LANES), I32)
    for t in range(16):
        count = jnp.where(tile == t, counts[t], count)
    live = position < count
    lin_x = con_a * x + con_b * y
    lin_y = con_b * x + con_c * y
    const = -0.5 * (x * lin_x + y * lin_y) - jnp.log(1.0 + jnp.exp(-logit))
    factors = [const, lin_x, lin_y, -0.5 * con_a, -con_b, -0.5 * con_c]
    for k, value in enumerate(factors):
        value = jnp.where(live, value * LOG2E, -1000.0 if k == 0 else 0.0)
        for p, part in enumerate(split3(value)):
            row = (p * 6 + k) * 32
            factor[row : row + 32, :] = part.astype(F32)
    for ch in range(3):
        for p, part in enumerate(split3(entry[192 + ch * 32 : 224 + ch * 32])):
            row = (18 + p * 3 + ch) * 32
            factor[row : row + 32, :] = part.astype(F32)
    factor[27 * 32 : 32 * 32, :] = jnp.zeros((5 * 32, LANES), F32)


def alphas_and_colors(factor, power, alpha, shade):
    def step(q, _):
        first = pl.multiple_of(q * LANES, LANES)
        left = factor[pl.ds(q, 32, stride=32), :].T.astype(BF16)
        out = dot_nn(left, power[...])
        alpha[pl.ds(first, LANES), :] = jnp.minimum(jnp.exp2(out[:, 0:256]), 0.99)
        shade[pl.ds(first, LANES), :] = out[:, 256:640]
        return 0

    lax.fori_loop(0, STEPS, step, 0, unroll=2)


def composite(alpha, shade, image):
    one = jnp.ones((16, LANES), F32)
    zero = jnp.zeros((16, LANES), F32)

    def step(q, state):
        through = list(state[0:2])
        total = list(state[2:8])
        for k in range(8):
            row = pl.ds(pl.multiple_of(q * LANES + k * 16, 16), 16)
            colors = [shade[row, ch * 128 : ch * 128 + 128] for ch in range(3)]
            for h in range(2):
                weight = alpha[row, h * 128 : h * 128 + 128] * through[h]
                through[h] = through[h] - weight
                for ch in range(3):
                    total[ch * 2 + h] = total[ch * 2 + h] + weight * colors[ch]
        return tuple(through + total)

    state = lax.fori_loop(0, STEPS, step, (one, one) + (zero,) * 6)
    for ch in range(3):
        for h in range(2):
            image[ch, :, h * 128 : h * 128 + 128] = state[2 + ch * 2 + h]


def weights_forward(alpha, weights):
    one = jnp.ones((16, LANES), F32)

    def step(q, through):
        through = list(through)
        for k in range(8):
            row = pl.ds(pl.multiple_of(q * LANES + k * 16, 16), 16)
            for h in range(2):
                weight = alpha[row, h * 128 : h * 128 + 128] * through[h]
                through[h] = through[h] - weight
                weights[row, h * 128 : h * 128 + 128] = weight
        return tuple(through)

    lax.fori_loop(0, STEPS, step, (one, one))


def backward(alpha, shade, weights, cot, pull, held):
    up = [cot[ch, :, h * 128 : h * 128 + 128] for ch in range(3) for h in range(2)]
    zero = jnp.zeros((16, LANES), F32)

    def step(s, behind):
        behind = list(behind)
        q = STEPS - 1 - s
        for k in range(7, -1, -1):
            row = pl.ds(pl.multiple_of(q * LANES + k * 16, 16), 16)
            colors = [shade[row, ch * 128 : ch * 128 + 128] for ch in range(3)]
            for h in range(2):
                opaque = alpha[row, h * 128 : h * 128 + 128]
                weight = weights[row, h * 128 : h * 128 + 128]
                value = up[h] * colors[0] + up[2 + h] * colors[1] + up[4 + h] * colors[2]
                ahead = value - behind[h]
                behind[h] = behind[h] + opaque * ahead
                pulled = jnp.where(opaque < 0.99, weight * ahead, 0.0)
                high, low = split2(pulled)
                pull[row, h * 128 : h * 128 + 128] = high
                pull[row, 256 + h * 128 : 384 + h * 128] = low
                high, low = split2(weight)
                held[row, h * 128 : h * 128 + 128] = high
                held[row, 256 + h * 128 : 384 + h * 128] = low
        return tuple(behind)

    lax.fori_loop(0, STEPS, step, (zero, zero))


def pixel_sums(pull, held, moments, cot, cots, sums):
    flat = cot[...].reshape(48, 256)
    high, low = split2(flat)
    cots[:, 0:256] = high
    cots[:, 256:512] = high
    cots[:, 512:768] = low
    own = iota((16, LANES), 0) == iota((16, LANES), 1) % 16

    def step(q, _):
        row = pl.ds(pl.multiple_of(q * LANES, LANES), LANES)
        moment = dot_nt(moments[...], pull[row, :])
        for v in range(6):
            sums[pl.ds(v * 32 + q, 1), :] = moment[v : v + 1]
        both = held[row, :]
        spread = dot_nt(cots[...], jnp.concatenate([both, both[:, 0:256]], 1))
        for ch in range(3):
            kept = jnp.where(own, spread[ch * 16 : ch * 16 + 16], 0.0)
            sums[pl.ds((6 + ch) * 32 + q, 1), :] = jnp.sum(kept, axis=0, keepdims=True)
        return 0

    lax.fori_loop(0, STEPS, step, 0, unroll=2)


def entry_gradients(entry, sums, grad):
    x = entry[0:32] - 8.0
    y = entry[32:64] - 8.0
    con_a = entry[64:96]
    con_b = entry[96:128]
    con_c = entry[128:160]
    fade = jnp.exp(-entry[160:192])
    s_0 = sums[0:32]
    s_x = sums[32:64]
    s_y = sums[64:96]
    d_x = s_x - x * s_0
    d_y = s_y - y * s_0
    d_xx = sums[96:128] - x * (s_x + d_x)
    d_xy = sums[128:160] - x * s_y - y * d_x
    d_yy = sums[160:192] - y * (s_y + d_y)
    values = [
        con_a * d_x + con_b * d_y,
        con_b * d_x + con_c * d_y,
        -0.5 * d_xx,
        -d_xy,
        -0.5 * d_yy,
        s_0 * (fade / (1.0 + fade)),
        sums[192:224],
        sums[224:256],
        sums[256:288],
    ]
    for v, value in enumerate(values):
        grad[v * 32 : v * 32 + 32, :] = value


def slots_in_order(grad, hot, slots, spread, msg):
    rows = iota((SLOTS, LANES), 0)

    def step(q, _):
        first = pl.multiple_of(q * LANES, LANES)
        here = rows == slots[pl.ds(q, 1), :] % SLOTS
        for v in range(9):
            value = grad[pl.ds(v * 32 + q, 1), :]
            high, low = split2(jnp.where(here, value, 0.0))
            spread[v * 32 : v * 32 + 32, pl.ds(first, LANES)] = high
            spread[288 + v * 32 : 320 + v * 32, pl.ds(first, LANES)] = low
        return 0

    lax.fori_loop(0, STEPS, step, 0, unroll=2)
    for g, size in ((0, 128), (1, 128), (2, 32)):
        high = dot_nt(hot[...], spread[g * 128 : g * 128 + size, :])
        low = dot_nt(hot[...], spread[288 + g * 128 : 288 + g * 128 + size, :])
        msg[:, 0, g * 128 : g * 128 + size] = high + low


def render_kernel(
    got_next, got_cur, hot_next, hot_cur, slots_next, slots_cur, counts_next, counts_cur, cot, power, moments,
    image, msg,
    split, entry, factor, alpha, shade, weights, pull, held, cots, sums, grad, spread,
):
    entries_in_order(got_cur, hot_cur, slots_cur, split, entry)
    power_factors(entry, counts_cur, factor)
    alphas_and_colors(factor, power, alpha, shade)
    weights_forward(alpha, weights)
    backward(alpha, shade, weights, cot, pull, held)
    pixel_sums(pull, held, moments, cot, cots, sums)
    entry_gradients(entry, sums, grad)
    slots_in_order(grad, hot_cur, slots_cur, spread, msg)
    msg[:, 0, 288:384] = jnp.zeros((N_DEV, 96), F32)
    entries_in_order(got_next, hot_next, slots_next, split, entry)
    power_factors(entry, counts_next, factor)
    alphas_and_colors(factor, power, alpha, shade)
    composite(alpha, shade, image)


def scatter_kernel(got, basis, sends, grads, turned, row_v, half, row_s, total, piece, rows, sem):
    split_index(sends, row_v, half)
    copy = pltpu.make_async_copy(row_v, row_s, sem)
    copy.start()
    for g in range(3):
        turned[g * 128 : g * 128 + 128, :] = got[:, 0, g * 128 : g * 128 + 128].T

    def clear(b, _):
        total[pl.ds(pl.multiple_of(b * 256, 256), 256), :] = jnp.zeros((256, LANES), F32)
        return 0

    lax.fori_loop(0, HALF // 256, clear, 0)
    piece[48:64, :] = jnp.zeros((16, LANES), F32)
    same_group = iota((LANES, LANES), 0) // 16 == iota((LANES, LANES), 1) // 16
    copy.wait()

    def slot(r, _):
        piece[0:6, :] = turned[pl.ds(r, 8, stride=32), :][0:6]
        terms = basis[pl.ds(r, 16, stride=32), :]
        for ch in range(3):
            piece[6 + 16 * ch : 22 + 16 * ch, :] = terms * turned[pl.ds((6 + ch) * 32 + r, 1), :]
        upper = half[pl.ds(r, 1), :] > 0.5
        values = piece[...]
        both = jnp.concatenate([jnp.where(upper, 0.0, values), jnp.where(upper, values, 0.0)], 0)
        high, low = split2(both)
        name = jnp.broadcast_to(row_v[pl.ds(r, 1), :].astype(F32), (LANES, LANES))
        same = jnp.logical_and(name == name.T, same_group).astype(F32).astype(BF16)
        rows[...] = dot_nt(jnp.concatenate([same, same], 1), jnp.concatenate([high, low], 1))
        for g in range(8):
            places = [row_s[r, g * 16 + u] for u in range(16)]
            olds = [total[pl.ds(places[u], 1), :] for u in range(16)]
            for u in range(16):
                total[pl.ds(places[u], 1), :] = olds[u] + rows[g * 16 + u : g * 16 + u + 1, :]
        return 0

    lax.fori_loop(0, SLOTS, slot, 0)

    def block(b, _):
        first = pl.multiple_of(b * LANES, LANES)
        both = total[pl.ds(first, LANES), :].T
        grads[:, pl.ds(first, LANES)] = both[0:ROWS]
        grads[:, pl.ds(first + HALF, LANES)] = both[64 : 64 + ROWS]
        return 0

    lax.fori_loop(0, HALF // LANES, block, 0, unroll=4)


VM = pl.BlockSpec(memory_space=pltpu.VMEM)
SM = pl.BlockSpec(memory_space=pltpu.SMEM)
PARAMS = pltpu.CompilerParams(vmem_limit_bytes=VMEM_LIMIT)


def shape(dims, dtype=F32):
    return jax.ShapeDtypeStruct(dims, dtype)


def exchange(x):
    return lax.all_to_all(x, AXES, split_axis=0, concat_axis=0, tiled=True)


def body(params, angles_next, angles_cur, lists_next, lists_cur, counts_next, counts_cur, sends_next, sends_cur, cotangent):
    power, moments = pixel_tables()
    hots = (N_DEV, 4096)
    dense = (STEPS, LANES)
    msg, slots_next, slots_cur, hot_next, hot_cur = pl.pallas_call(
        lists_kernel,
        out_shape=(shape((N_DEV, 1, 128)), shape(dense, I32), shape(dense, I32), shape(hots, BF16), shape(hots, BF16)),
        in_specs=[VM, VM, SM, SM],
        out_specs=(VM,) * 5,
        scratch_shapes=[pltpu.VMEM((256, LANES), F32), pltpu.VMEM((SLOTS, 4096), BF16)],
        compiler_params=PARAMS,
        name="lists",
    )(lists_next, lists_cur, angles_next, angles_cur)
    angles = exchange(msg)
    msg_next, msg_cur, basis = pl.pallas_call(
        owner_kernel,
        out_shape=(shape((N_DEV, 1, 384)), shape((N_DEV, 1, 384)), shape((512, LANES))),
        in_specs=[VM, VM, VM, VM],
        out_specs=(VM,) * 3,
        scratch_shapes=[
            pltpu.VMEM((HALF, LANES), F32),
            pltpu.VMEM((256, LANES), F32),
            pltpu.VMEM((SLOTS * 64, LANES), F32),
            pltpu.VMEM(dense, I32),
            pltpu.VMEM(dense, F32),
            pltpu.VMEM(dense, F32),
            pltpu.SMEM(dense, I32),
            pltpu.SMEM(dense, I32),
            pltpu.VMEM((512, LANES), F32),
            pltpu.VMEM((96, LANES), F32),
            pltpu.SemaphoreType.DMA,
        ],
        compiler_params=PARAMS,
        name="owner",
    )(params, sends_next[0], sends_cur[0], angles)
    got_cur = exchange(msg_cur)
    got_next = exchange(msg_next)
    image, msg = pl.pallas_call(
        render_kernel,
        out_shape=(shape((3, 16, 256)), shape((N_DEV, 1, 384))),
        in_specs=[VM] * 6 + [SM, SM] + [VM] * 3,
        out_specs=(VM,) * 2,
        scratch_shapes=[
            pltpu.VMEM((288, 384), BF16),
            pltpu.VMEM((288, LANES), F32),
            pltpu.VMEM((1024, LANES), F32),
            pltpu.VMEM((4096, 256), F32),
            pltpu.VMEM((4096, 384), F32),
            pltpu.VMEM((4096, 256), F32),
            pltpu.VMEM((4096, 512), BF16),
            pltpu.VMEM((4096, 512), BF16),
            pltpu.VMEM((48, 768), BF16),
            pltpu.VMEM((288, LANES), F32),
            pltpu.VMEM((288, LANES), F32),
            pltpu.VMEM((576, 4096), BF16),
        ],
        compiler_params=PARAMS,
        name="render",
    )(got_next, got_cur, hot_next, hot_cur, slots_next, slots_cur, counts_next, counts_cur,
      jnp.transpose(cotangent, (1, 0, 2)), power, moments)
    got = exchange(msg)
    grads = pl.pallas_call(
        scatter_kernel,
        out_shape=shape((ROWS, GAUSS)),
        in_specs=[VM] * 3,
        out_specs=VM,
        scratch_shapes=[
            pltpu.VMEM((384, LANES), F32),
            pltpu.VMEM(dense, I32),
            pltpu.VMEM(dense, F32),
            pltpu.SMEM(dense, I32),
            pltpu.VMEM((HALF, LANES), F32),
            pltpu.VMEM((64, LANES), F32),
            pltpu.VMEM((LANES, LANES), F32),
            pltpu.SemaphoreType.DMA,
        ],
        compiler_params=PARAMS,
        name="scatter",
    )(got, basis, sends_cur[0])
    return jnp.transpose(image, (1, 0, 2)), grads


def solution(mesh):
    both = ("gauss", "pix")
    placed = (
        P(None, both),
        P(both, None),
        P(both, None),
        P(both, None),
        P(both, None),
        P(both),
        P(both),
        P(both, None, None),
        P(both, None, None),
        P(both, None, None),
    )
    return jax.shard_map(
        body,
        mesh=mesh,
        in_specs=placed,
        out_specs=(P(both, None, None), P(None, both)),
        check_vma=False,
    )
```

profile of v0, /device:TPU:1, one launch (start us, length us, event | category | flops | bytes accessed | tf_op | source)
XLA Modules:
  0.0 147.6 jit_solution(12461908738358412513)
XLA Ops:
  0.6 1.4 copy.16.angles_next
  2.0 1.4 copy.17.angles_cur
  3.3 4.0 %lists.1 = (f32[128,1,128]{2,1,0:T(1,128)}, s32[32,128]{1,0:T(8,128)}, s32[32,128]{1,0:T(8,128)}, bf16[128,4096]{1,0:T(8,128)(2,1)}, bf16[128,4096]{1,0:T(8,128)(2,1)}) custom-call(s32[16,256]{1,0:T(8,128)} %lists_next.1, s32[16,256]{1,0:T(8,128)} %lists_cur.1, f32[16,2]{1,0:T(8,128)} %copy.16.angles_next, f32[16,2]{1,0:T(8,128)} %copy.17.angles_cur), custom_call_target="tpu_custom_call" | custom-call | tf_op jit(solution)/shard_map/lists/pallas_call | solution.py:509
  7.4 11.5 %all-to-all-start = ((f32[128,1,128]{2,1,0:T(1,128)}), f32[128,1,128]{2,1,0:T(1,128)S(1)}, u32[]{:S(2)}, u32[]{:S(2)}) async-start(f32[128,1,128]{2,1,0:T(1,128)} %get-tuple-element.12), calls=%async_computation | async-start | bytes 131072 | tf_op jit(solution)/shard_map/all_to_all | solution.py:502
  18.9 1.4 copy.14
  20.3 1.4 copy.15
  21.7 6.5 %all-to-all-done.angles = f32[128,1,128]{2,1,0:T(1,128)S(1)} async-done(((f32[128,1,128]{2,1,0:T(1,128)}), f32[128,1,128]{2,1,0:T(1,128)S(1)}, u32[]{:S(2)}, u32[]{:S(2)}) %all-to-all-start) | async-done | bytes 65568 | tf_op jit(solution)/shard_map/all_to_all | solution.py:502
  28.2 0.0 copy-start
  28.2 0.6 copy-done
  28.9 18.4 %owner.1 = (f32[128,1,384]{2,1,0:T(1,128)}, f32[128,1,384]{2,1,0:T(1,128)}, f32[512,128]{1,0:T(8,128)}) custom-call(f32[54,16384]{1,0:T(8,128)} %params.1, s32[128,32]{1,0:T(8,128)} %bitcast.6, s32[128,32]{1,0:T(8,128)} %bitcast.4, f32[128,1,128]{2,1,0:T(1,128)} %copy-done), custom_call_target="tpu_custom_call" | custom-call | tf_op jit(solution)/shard_map/owner/pallas_call | solution.py:519
  47.3 16.1 %all_to_all.20.got_next = f32[128,1,384]{2,1,0:T(1,128)} all-to-all(f32[128,1,384]{2,1,0:T(1,128)} %get-tuple-element.13), channel_id=1, replica_groups=mesh['gauss'=4,'pix'=32] {'gauss','pix'}, dimensions={0} | all-to-all | bytes 393216 | tf_op jit(solution)/shard_map/all_to_all | solution.py:502
  63.4 15.7 %all_to_all.21.got_cur = f32[128,1,384]{2,1,0:T(1,128)} all-to-all(f32[128,1,384]{2,1,0:T(1,128)} %get-tuple-element.14), channel_id=1, replica_groups=mesh['gauss'=4,'pix'=32] {'gauss','pix'}, dimensions={0} | all-to-all | bytes 393216 | tf_op jit(solution)/shard_map/all_to_all | solution.py:502
  79.1 36.0 %render.1 = (f32[3,16,256]{2,1,0:T(8,128)}, f32[128,1,384]{2,1,0:T(1,128)}) custom-call(f32[128,1,384]{2,1,0:T(1,128)} %all_to_all.20.got_next, f32[128,1,384]{2,1,0:T(1,128)} %all_to_all.21.got_cur, bf16[128,4096]{1,0:T(8,128)(2,1)} %get-tuple-element.15.hot_next, bf16[128,4096]{1,0:T(8,128)(2,1)} %get-tuple-element.16.hot_cur, ...), custom_call_target="tpu_custom_call" | custom-call | tf_op jit(solution)/shard_map/render/pallas_call | solution.py:542
  115.1 15.6 %all_to_all.22.got = f32[128,1,384]{2,1,0:T(1,128)} all-to-all(f32[128,1,384]{2,1,0:T(1,128)} %get-tuple-element.20), channel_id=1, replica_groups=mesh['gauss'=4,'pix'=32] {'gauss','pix'}, dimensions={0} | all-to-all | bytes 393216 | tf_op jit(solution)/shard_map/all_to_all | solution.py:502
  130.7 16.9 %scatter.1 = f32[54,16384]{1,0:T(8,128)} custom-call(f32[128,1,384]{2,1,0:T(1,128)} %all_to_all.22.got, f32[512,128]{1,0:T(8,128)} %get-tuple-element.21.basis, s32[128,32]{1,0:T(8,128)} %bitcast.5), custom_call_target="tpu_custom_call" | custom-call | tf_op jit(solution)/shard_map/scatter/pallas_call | solution.py:566
Async XLA Ops:
  7.4 20.9 %all-to-all-start = ((f32[128,1,128]{2,1,0:T(1,128)}), f32[128,1,128]{2,1,0:T(1,128)S(1)}, u32[]{:S(2)}, u32[]{:S(2)}) async-start(f32[128,1,128]{2,1,0:T(1,128)} %get-tuple-element.12), calls=%async_computation | async-start | bytes 131072 | tf_op jit(solution)/shard_map/all_to_all | solution.py:502
  28.2 0.6 copy-start
where the time goes:
time: 148 us
  Pallas kernels  75.3 us (51%)
  blocking collectives  47.5 us (32%)
  starting transfers between devices  11.5 us (8%)
  waiting for transfers between devices  6.48 us (4%)
  local copies, waits for them, and re-layouts  6.19 us (4%)
    all_to_all x3, blocking collectives, exchange(): return lax.all_to_all(x, AXES, split_axis=0, concat_axis=0, tiled=True)  47.5 us
    pallas_call x1, Pallas kernels, body(): pl.pallas_call(render_kernel, out_shape=(shape((3, 16, 256)), shape((N_DE...  36 us
    pallas_call x1, Pallas kernels, body(): pl.pallas_call(owner_kernel, out_shape=(shape((N_DEV, 1, 384)), shape((N_...  18.4 us
    pallas_call x1, Pallas kernels, body(): pl.pallas_call(scatter_kernel, out_shape=shape((ROWS, GAUSS)), in_specs=[...  16.9 us
    all_to_all x1, starting transfers between devices, exchange(): return lax.all_to_all(x, AXES, split_axis=0, concat_axis=0, tiled=True)  11.5 us
    all_to_all x1, waiting for transfers between devices, exchange(): return lax.all_to_all(x, AXES, split_axis=0, concat_axis=0, tiled=True)  6.48 us
    unnamed x6, local copies, waits for them, and re-layouts  6.19 us
    pallas_call x1, Pallas kernels, body(): pl.pallas_call(lists_kernel, out_shape=(shape((N_DEV, 1, 128)), shape(den...  4.04 us
  transfers between devices with their start and end apart: 1, of which 1 were waited for; matrix products, arithmetic and copies ran while one was open for 2% of the time, Pallas kernels for 0%

commit v1 on v0

--- a/solution.py
+++ b/solution.py
@@ -9,12 +9,13 @@
 F32 = jnp.float32
 BF16 = jnp.bfloat16
 I32 = jnp.int32
-AXES = ("gauss", "pix")
+MESH = pl.DeviceIdType.MESH
 N_DEV = 128
 N_PIX = 32
 SLOTS = 32
 GAUSS = 16384
 HALF = 8192
+CHUNKS = 4
 ROWS = 54
 LANES = 128
 STEPS = 32
@@ -65,13 +66,13 @@
 
 
 def order_lists(lists_ref, turned, slots_ref):
-    turned[:, 0:16] = lists_ref[...].astype(F32).T
+    turned[0:256, 0:16] = lists_ref[...].T
     lane_group = iota((STEPS, LANES), 1) // 16
-    out = jnp.zeros((STEPS, LANES), F32)
+    out = jnp.zeros((STEPS, LANES), I32)
     for k in range(8):
         piece = pltpu.roll(turned[pl.ds(k, STEPS, stride=8), :], 16 * k, 1) if k else turned[pl.ds(0, STEPS, stride=8), :]
         out = jnp.where(lane_group == k, piece, out)
-    slots_ref[...] = out.astype(I32)
+    slots_ref[...] = out
 
 
 def owner_onehot(slots_ref, hot_ref):
@@ -102,16 +103,6 @@
         )
         out = jnp.where(tiles == float(t), row, out)
     return out
-
-
-def lists_kernel(lists_next, lists_cur, angles_next, angles_cur, msg, slots_next, slots_cur, hot_next, hot_cur, turned, mark):
-    order_lists(lists_next, turned, slots_next)
-    owner_onehot(slots_next, hot_next)
-    tiles_next = slot_tiles(slots_next, hot_next, mark)
-    order_lists(lists_cur, turned, slots_cur)
-    owner_onehot(slots_cur, hot_cur)
-    tiles_cur = slot_tiles(slots_cur, hot_cur, mark)
-    msg[:, 0, :] = angle_message(tiles_next, tiles_cur, angles_next, angles_cur)
 
 
 def sh_terms(theta, azimuth):
@@ -142,18 +133,33 @@
     ]
 
 
-def build_table(params, table):
+def param_copies(params, held, sems):
+    width = HALF // CHUNKS
+    out = []
+    for c in range(CHUNKS):
+        for k in range(2):
+            cols = pl.ds(k * HALF + c * width, width)
+            out.append(pltpu.make_async_copy(params.at[:, cols], held.at[:, cols], sems.at[c * 2 + k]))
+    return out
+
+
+def build_table(copies, params, table):
     zeros = jnp.zeros((64 - ROWS, LANES), F32)
-
-    def block(b, _):
-        first = pl.multiple_of(b * LANES, LANES)
-        both = jnp.concatenate(
-            [params[:, pl.ds(first, LANES)], zeros, params[:, pl.ds(first + HALF, LANES)], zeros], 0
-        )
-        table[pl.ds(first, LANES), :] = both.T
-        return 0
-
-    lax.fori_loop(0, HALF // LANES, block, 0, unroll=4)
+    blocks = HALF // LANES // CHUNKS
+
+    for c in range(CHUNKS):
+        copies[c * 2].wait()
+        copies[c * 2 + 1].wait()
+
+        def block(b, _):
+            first = pl.multiple_of((c * blocks + b) * LANES, LANES)
+            both = jnp.concatenate(
+                [params[:, pl.ds(first, LANES)], zeros, params[:, pl.ds(first + HALF, LANES)], zeros], 0
+            )
+            table[pl.ds(first, LANES), :] = both.T
+            return 0
+
+        lax.fori_loop(0, blocks, block, 0, unroll=8)
 
 
 def gather_rows(index, table, rows, half_ref, turned):
@@ -163,7 +169,7 @@
         for k in range(2):
             r = r2 * 2 + k
             both = rows[k * 128 : k * 128 + 128, :].T
-            upper = half_ref[pl.ds(r, 1), :] > 0.5
+            upper = half_ref[pl.ds(r, 1), :] > 0
             turned[pl.ds(pl.multiple_of(r * 64, 64), 64), :] = jnp.where(upper, both[64:], both[:64])
         return 0
 
@@ -171,10 +177,9 @@
 
 
 def split_index(sends_ref, row_ref, half_ref):
-    turned = sends_ref[...].astype(F32).T
-    upper = turned >= float(HALF)
-    half_ref[...] = upper.astype(F32)
-    row_ref[...] = jnp.where(upper, turned - float(HALF), turned).astype(I32)
+    turned = sends_ref[...].T
+    half_ref[...] = turned // HALF
+    row_ref[...] = turned % HALF
 
 
 def color_rows(basis, turned, color):
@@ -194,32 +199,6 @@
     msg[:, 0, 128:256] = jnp.concatenate([geo[4], geo[5], color[0:32], color[32:64]], 0).T
     last = color[64:96]
     msg[:, 0, 256:384] = jnp.concatenate([last, last, last, last], 0).T
-
-
-def owner_kernel(
-    params, sends_next, sends_cur, angles, msg_next, msg_cur, basis_cur,
-    table, rows, turned, row_v, half_next, half_cur, row_next, row_cur, basis_next, color, sem,
-):
-    split_index(sends_next, row_v, half_next)
-    copy = pltpu.make_async_copy(row_v, row_next, sem)
-    copy.start()
-    copy.wait()
-    split_index(sends_cur, row_v, half_cur)
-    copy = pltpu.make_async_copy(row_v, row_cur, sem)
-    copy.start()
-    copy.wait()
-    build_table(params, table)
-    seen = angles[:, 0, :].T
-    for k, term in enumerate(sh_terms(seen[0:32], seen[32:64])):
-        basis_next[k * 32 : k * 32 + 32, :] = term
-    for k, term in enumerate(sh_terms(seen[64:96], seen[96:128])):
-        basis_cur[k * 32 : k * 32 + 32, :] = term
-    gather_rows(row_cur, table, rows, half_cur, turned)
-    color_rows(basis_cur, turned, color)
-    owner_message(turned, color, msg_cur)
-    gather_rows(row_next, table, rows, half_next, turned)
-    color_rows(basis_next, turned, color)
-    owner_message(turned, color, msg_next)
 
 
 def entries_in_order(got, hot, slots, split, entry):
@@ -422,11 +401,107 @@
         msg[:, 0, g * 128 : g * 128 + size] = high + low
 
 
-def render_kernel(
-    got_next, got_cur, hot_next, hot_cur, slots_next, slots_cur, counts_next, counts_cur, cot, power, moments,
-    image, msg,
+def place_of(device):
+    return (device // N_PIX, lax.rem(device, N_PIX))
+
+
+def greet(me):
+    barrier = pltpu.get_barrier_semaphore()
+
+    def one(k, _):
+        pl.semaphore_signal(barrier, inc=1, device_id=place_of(lax.rem(me + k, N_DEV)), device_id_type=MESH)
+        return 0
+
+    lax.fori_loop(1, N_DEV, one, 0)
+
+
+def await_greetings():
+    pl.semaphore_wait(pltpu.get_barrier_semaphore(), N_DEV - 1)
+
+
+def send_all(me, msg, got, send_sem, recv_sem):
+    def one(k, _):
+        there = lax.rem(me + k, N_DEV)
+        pltpu.make_async_remote_copy(
+            src_ref=msg.at[there],
+            dst_ref=got.at[me],
+            send_sem=send_sem,
+            recv_sem=recv_sem,
+            device_id=place_of(there),
+            device_id_type=MESH,
+        ).start()
+        return 0
+
+    lax.fori_loop(1, N_DEV, one, 0)
+    got[me] = msg[me]
+
+
+def all_of(me, msg, got, send_sem, recv_sem):
+    return pltpu.make_async_remote_copy(
+        src_ref=msg.at[pl.ds(0, N_DEV - 1)],
+        dst_ref=got.at[pl.ds(0, N_DEV - 1)],
+        send_sem=send_sem,
+        recv_sem=recv_sem,
+        device_id=place_of(lax.rem(me + 1, N_DEV)),
+        device_id_type=MESH,
+    )
+
+
+def main_kernel(
+    params, lists_next, lists_cur, angles_next, angles_cur, counts_next, counts_cur,
+    sends_next, sends_cur, cot, power, moments,
+    image, returned, basis_cur,
+    ask, asked, msg_cur, got_cur, msg_next, got_next, back, got_back,
+    slots_next, slots_cur, hot_next, hot_cur, turned, mark,
+    held_params, table, rows, rows_cur, rows_next, row_v, half_next, half_cur, row_next, row_cur, basis_next, color,
     split, entry, factor, alpha, shade, weights, pull, held, cots, sums, grad, spread,
+    send_sems, recv_sems, param_sems, index_sems,
 ):
+    me = lax.axis_index("gauss") * N_PIX + lax.axis_index("pix")
+    greet(me)
+    copies = param_copies(params, held_params, param_sems)
+    for copy in copies:
+        copy.start()
+    split_index(sends_cur, row_v.at[0], half_cur)
+    split_index(sends_next, row_v.at[1], half_next)
+    to_smem = [
+        pltpu.make_async_copy(row_v.at[0], row_cur, index_sems.at[0]),
+        pltpu.make_async_copy(row_v.at[1], row_next, index_sems.at[1]),
+    ]
+    for copy in to_smem:
+        copy.start()
+    order_lists(lists_next, turned, slots_next)
+    owner_onehot(slots_next, hot_next)
+    tiles_next = slot_tiles(slots_next, hot_next, mark)
+    order_lists(lists_cur, turned, slots_cur)
+    owner_onehot(slots_cur, hot_cur)
+    tiles_cur = slot_tiles(slots_cur, hot_cur, mark)
+    ask[:, 0, :] = angle_message(tiles_next, tiles_cur, angles_next, angles_cur)
+    await_greetings()
+    links = [
+        (me, src, dst, send_sems.at[k], recv_sems.at[k])
+        for k, (src, dst) in enumerate(((ask, asked), (msg_cur, got_cur), (msg_next, got_next), (back, got_back)))
+    ]
+    send_all(*links[0])
+    for copy in to_smem:
+        copy.wait()
+    build_table(copies, held_params, table)
+    gather_rows(row_cur, table, rows, half_cur, rows_cur)
+    all_of(*links[0]).wait_recv()
+    seen = asked[:, 0, :].T
+    for k, term in enumerate(sh_terms(seen[64:96], seen[96:128])):
+        basis_cur[k * 32 : k * 32 + 32, :] = term
+    color_rows(basis_cur, rows_cur, color)
+    owner_message(rows_cur, color, msg_cur)
+    basis_cur[512:544, :] = jnp.zeros((32, LANES), F32)
+    send_all(*links[1])
+    for k, term in enumerate(sh_terms(seen[0:32], seen[32:64])):
+        basis_next[k * 32 : k * 32 + 32, :] = term
+    gather_rows(row_next, table, rows, half_next, rows_next)
+    color_rows(basis_next, rows_next, color)
+    owner_message(rows_next, color, msg_next)
+    send_all(*links[2])
+    all_of(*links[1]).wait_recv()
     entries_in_order(got_cur, hot_cur, slots_cur, split, entry)
     power_factors(entry, counts_cur, factor)
     alphas_and_colors(factor, power, alpha, shade)
@@ -434,20 +509,25 @@
     backward(alpha, shade, weights, cot, pull, held)
     pixel_sums(pull, held, moments, cot, cots, sums)
     entry_gradients(entry, sums, grad)
-    slots_in_order(grad, hot_cur, slots_cur, spread, msg)
-    msg[:, 0, 288:384] = jnp.zeros((N_DEV, 96), F32)
+    slots_in_order(grad, hot_cur, slots_cur, spread, back)
+    back[:, 0, 288:384] = jnp.zeros((N_DEV, 96), F32)
+    send_all(*links[3])
+    all_of(*links[2]).wait_recv()
     entries_in_order(got_next, hot_next, slots_next, split, entry)
     power_factors(entry, counts_next, factor)
     alphas_and_colors(factor, power, alpha, shade)
     composite(alpha, shade, image)
-
-
-def scatter_kernel(got, basis, sends, grads, turned, row_v, half, row_s, total, piece, rows, sem):
+    all_of(*links[3]).wait_recv()
+    for g in range(3):
+        returned[g * 128 : g * 128 + 128, :] = got_back[:, 0, g * 128 : g * 128 + 128].T
+    for link in links:
+        all_of(*link).wait_send()
+
+
+def scatter_kernel(turned, basis, sends, grads, row_v, half, row_s, total, piece, rows, sem):
     split_index(sends, row_v, half)
     copy = pltpu.make_async_copy(row_v, row_s, sem)
     copy.start()
-    for g in range(3):
-        turned[g * 128 : g * 128 + 128, :] = got[:, 0, g * 128 : g * 128 + 128].T
 
     def clear(b, _):
         total[pl.ds(pl.multiple_of(b * 256, 256), 256), :] = jnp.zeros((256, LANES), F32)
@@ -463,7 +543,7 @@
         terms = basis[pl.ds(r, 16, stride=32), :]
         for ch in range(3):
             piece[6 + 16 * ch : 22 + 16 * ch, :] = terms * turned[pl.ds((6 + ch) * 32 + r, 1), :]
-        upper = half[pl.ds(r, 1), :] > 0.5
+        upper = half[pl.ds(r, 1), :] > 0
         values = piece[...]
         both = jnp.concatenate([jnp.where(upper, 0.0, values), jnp.where(upper, values, 0.0)], 0)
         high, low = split2(both)
@@ -498,56 +578,40 @@
     return jax.ShapeDtypeStruct(dims, dtype)
 
 
-def exchange(x):
-    return lax.all_to_all(x, AXES, split_axis=0, concat_axis=0, tiled=True)
-
-
 def body(params, angles_next, angles_cur, lists_next, lists_cur, counts_next, counts_cur, sends_next, sends_cur, cotangent):
     power, moments = pixel_tables()
-    hots = (N_DEV, 4096)
     dense = (STEPS, LANES)
-    msg, slots_next, slots_cur, hot_next, hot_cur = pl.pallas_call(
-        lists_kernel,
-        out_shape=(shape((N_DEV, 1, 128)), shape(dense, I32), shape(dense, I32), shape(hots, BF16), shape(hots, BF16)),
-        in_specs=[VM, VM, SM, SM],
-        out_specs=(VM,) * 5,
-        scratch_shapes=[pltpu.VMEM((256, LANES), F32), pltpu.VMEM((SLOTS, 4096), BF16)],
-        compiler_params=PARAMS,
-        name="lists",
-    )(lists_next, lists_cur, angles_next, angles_cur)
-    angles = exchange(msg)
-    msg_next, msg_cur, basis = pl.pallas_call(
-        owner_kernel,
-        out_shape=(shape((N_DEV, 1, 384)), shape((N_DEV, 1, 384)), shape((512, LANES))),
-        in_specs=[VM, VM, VM, VM],
+    wide = pltpu.VMEM((N_DEV, 1, 384), F32)
+    image, returned, basis = pl.pallas_call(
+        main_kernel,
+        out_shape=(shape((3, 16, 256)), shape((384, LANES)), shape((544, LANES))),
+        in_specs=[pl.BlockSpec(memory_space=pl.ANY), VM, VM, SM, SM, SM, SM, VM, VM, VM, VM, VM],
         out_specs=(VM,) * 3,
         scratch_shapes=[
+            pltpu.VMEM((N_DEV, 1, 128), F32),
+            pltpu.VMEM((N_DEV, 1, 128), F32),
+            wide, wide, wide, wide, wide, wide,
+            pltpu.VMEM(dense, I32),
+            pltpu.VMEM(dense, I32),
+            pltpu.VMEM((N_DEV, 4096), BF16),
+            pltpu.VMEM((N_DEV, 4096), BF16),
+            pltpu.VMEM((264, LANES), I32),
+            pltpu.VMEM((SLOTS, 4096), BF16),
+            pltpu.VMEM((ROWS, GAUSS), F32),
             pltpu.VMEM((HALF, LANES), F32),
             pltpu.VMEM((256, LANES), F32),
-            pltpu.VMEM((SLOTS * 64, LANES), F32),
+            pltpu.VMEM((SLOTS * 64 + 8, LANES), F32),
+            pltpu.VMEM((SLOTS * 64 + 8, LANES), F32),
+            pltpu.VMEM((2,) + dense, I32),
             pltpu.VMEM(dense, I32),
-            pltpu.VMEM(dense, F32),
-            pltpu.VMEM(dense, F32),
+            pltpu.VMEM(dense, I32),
             pltpu.SMEM(dense, I32),
             pltpu.SMEM(dense, I32),
-            pltpu.VMEM((512, LANES), F32),
+            pltpu.VMEM((544, LANES), F32),
             pltpu.VMEM((96, LANES), F32),
-            pltpu.SemaphoreType.DMA,
-        ],
-        compiler_params=PARAMS,
-        name="owner",
-    )(params, sends_next[0], sends_cur[0], angles)
-    got_cur = exchange(msg_cur)
-    got_next = exchange(msg_next)
-    image, msg = pl.pallas_call(
-        render_kernel,
-        out_shape=(shape((3, 16, 256)), shape((N_DEV, 1, 384))),
-        in_specs=[VM] * 6 + [SM, SM] + [VM] * 3,
-        out_specs=(VM,) * 2,
-        scratch_shapes=[
             pltpu.VMEM((288, 384), BF16),
             pltpu.VMEM((288, LANES), F32),
-            pltpu.VMEM((1024, LANES), F32),
+            pltpu.VMEM((1056, LANES), F32),
             pltpu.VMEM((4096, 256), F32),
             pltpu.VMEM((4096, 384), F32),
             pltpu.VMEM((4096, 256), F32),
@@ -557,21 +621,25 @@
             pltpu.VMEM((288, LANES), F32),
             pltpu.VMEM((288, LANES), F32),
             pltpu.VMEM((576, 4096), BF16),
+            pltpu.SemaphoreType.DMA((4,)),
+            pltpu.SemaphoreType.DMA((4,)),
+            pltpu.SemaphoreType.DMA((2 * CHUNKS,)),
+            pltpu.SemaphoreType.DMA((2,)),
         ],
-        compiler_params=PARAMS,
-        name="render",
-    )(got_next, got_cur, hot_next, hot_cur, slots_next, slots_cur, counts_next, counts_cur,
-      jnp.transpose(cotangent, (1, 0, 2)), power, moments)
-    got = exchange(msg)
+        compiler_params=pltpu.CompilerParams(
+            vmem_limit_bytes=VMEM_LIMIT, collective_id=0, has_side_effects=True
+        ),
+        name="main",
+    )(params, lists_next, lists_cur, angles_next, angles_cur, counts_next, counts_cur,
+      sends_next[0], sends_cur[0], jnp.transpose(cotangent, (1, 0, 2)), power, moments)
     grads = pl.pallas_call(
         scatter_kernel,
         out_shape=shape((ROWS, GAUSS)),
         in_specs=[VM] * 3,
         out_specs=VM,
         scratch_shapes=[
-            pltpu.VMEM((384, LANES), F32),
             pltpu.VMEM(dense, I32),
-            pltpu.VMEM(dense, F32),
+            pltpu.VMEM(dense, I32),
             pltpu.SMEM(dense, I32),
             pltpu.VMEM((HALF, LANES), F32),
             pltpu.VMEM((64, LANES), F32),
@@ -580,7 +648,7 @@
         ],
         compiler_params=PARAMS,
         name="scatter",
-    )(got, basis, sends_cur[0])
+    )(returned, basis, sends_cur[0])
     return jnp.transpose(image, (1, 0, 2)), grads
 
 

time: 148 us -> 95.7 us (0.65)
  blocking collectives: 47.5 us -> 0 us
  Pallas kernels: 75.3 us -> 88.5 us
  starting transfers between devices: 11.5 us -> 0 us
  waiting for transfers between devices: 6.48 us -> 0 us
    all_to_all x3 -> x0, blocking collectives: 47.5 us -> none  [exchange(): return lax.all_to_all(x, AXES, split_axis=0, concat_axis=0, tiled=True)]
    pallas_call x3 -> x1, Pallas kernels: 58.4 us -> 71.6 us  [body(): pl.pallas_call(main_kernel, out_shape=(shape((3, 16, 256)), shape((384, L...]
    all_to_all x1 -> x0, starting transfers between devices: 11.5 us -> none  [exchange(): return lax.all_to_all(x, AXES, split_axis=0, concat_axis=0, tiled=True)]
    all_to_all x1 -> x0, waiting for transfers between devices: 6.48 us -> none  [exchange(): return lax.all_to_all(x, AXES, split_axis=0, concat_axis=0, tiled=True)]
    unnamed x6 -> x7, local copies, waits for them, and re-layouts: 6.19 us -> 6.21 us
  transfers between devices with their start and end apart: 1 -> 0, of which waited for: 1 -> 0; matrix products, arithmetic and copies ran while one was open for 2% -> 0% of each run, Pallas kernels for 0% -> 0%
where the time goes in v1:
time: 95.7 us; the launch traced here: 95.4 us
  Pallas kernels  88.5 us (92%)
  local copies, waits for them, and re-layouts  6.21 us (6%)
    pallas_call x1, Pallas kernels, body(): pl.pallas_call(main_kernel, out_shape=(shape((3, 16, 256)), shape((384, L...  71.6 us
    pallas_call x1, Pallas kernels, body(): pl.pallas_call(scatter_kernel, out_shape=shape((ROWS, GAUSS)), in_specs=[...  16.9 us
    unnamed x7, local copies, waits for them, and re-layouts  6.21 us

profile of v1, /device:TPU:1, one launch (start us, length us, event | category | flops | bytes accessed | tf_op | source)
XLA Modules:
  0.0 95.4 jit_solution(18290741920501085900)
XLA Ops:
  0.6 1.4 %copy.16.angles_next = f32[16,2]{1,0:T(8,128)} copy(f32[16,2]{0,1:T(2,128)} %param.13) | data formatting | bytes 256 | tf_op args[1]
  2.0 1.3 %copy.17.angles_cur = f32[16,2]{1,0:T(8,128)} copy(f32[16,2]{0,1:T(2,128)} %param.14) | data formatting | bytes 256 | tf_op args[2]
  3.3 1.4 %copy.14 = s32[1,128,32]{2,1,0:T(8,128)} copy(s32[1,128,32]{1,2,0:T(8,128)} %param.19) | data formatting | bytes 32768 | tf_op args[7]
  4.8 1.4 %copy.15 = s32[1,128,32]{2,1,0:T(8,128)} copy(s32[1,128,32]{1,2,0:T(8,128)} %param.20) | data formatting | bytes 32768 | tf_op args[8]
  6.2 71.6 %main.1 = (f32[3,16,256]{2,1,0:T(8,128)}, f32[384,128]{1,0:T(8,128)}, f32[544,128]{1,0:T(8,128)}) custom-call(f32[54,16384]{1,0:T(8,128)} %params.1, s32[16,256]{1,0:T(8,128)} %lists_next.1, s32[16,256]{1,0:T(8,128)} %lists_cur.1, f32[16,2]{1,0:T(8,128)} %copy.16.angles_next, f32[16,2]{1,0:T(8,128)} %copy.17.angles_cur, s32[16]{0:T(128)} %counts_next.1, ...), custom_call_target="tpu_custom_call" | custom-call | tf_op jit(solution)/shard_map/main/pallas_call | solution.py:585
  77.9 0.0 copy-start
  77.9 16.9 %scatter.1 = f32[54,16384]{1,0:T(8,128)} custom-call(f32[384,128]{1,0:T(8,128)} %get-tuple-element.6.turned, f32[544,128]{1,0:T(8,128)} %get-tuple-element.7.basis, s32[128,32]{1,0:T(8,128)} %bitcast.5), custom_call_target="tpu_custom_call" | custom-call | tf_op jit(solution)/shard_map/scatter/pallas_call | solution.py:635
  94.8 0.0 copy-done
  94.8 0.6 copy.19
Async XLA Ops:
  77.9 16.9 %copy-start = (f32[3,16,256]{2,1,0:T(8,128)S(1)}, f32[3,16,256]{2,1,0:T(8,128)}, u32[]{:S(2)}) copy-start(f32[3,16,256]{2,1,0:T(8,128)} %get-tuple-element.5) | copy-start | bytes 147460

commit v2 on v1

--- a/solution.py
+++ b/solution.py
@@ -16,6 +16,9 @@
 GAUSS = 16384
 HALF = 8192
 CHUNKS = 4
+UNROLL_ENTRY = 8
+UNROLL_ALPHA = 8
+GROUP = 8
 ROWS = 54
 LANES = 128
 STEPS = 32
@@ -98,8 +101,8 @@
     for t in range(16):
         row = jnp.where(
             region < 2,
-            jnp.where(region == 0, angles_next[t, 0], angles_next[t, 1]),
-            jnp.where(region == 2, angles_cur[t, 0], angles_cur[t, 1]),
+            jnp.where(region == 0, angles_next[0, t], angles_next[1, t]),
+            jnp.where(region == 2, angles_cur[0, t], angles_cur[1, t]),
         )
         out = jnp.where(tiles == float(t), row, out)
     return out
@@ -163,21 +166,23 @@
 
 
 def gather_rows(index, table, rows, half_ref, turned):
-    def pair(r2, _):
-        for u in range(256):
-            rows[u : u + 1, :] = table[pl.ds(index[r2 * 2 + u // 128, u % 128], 1), :]
-        for k in range(2):
-            r = r2 * 2 + k
+    def some(step, _):
+        for k in range(GROUP):
+            for d in range(LANES):
+                place = index[step * GROUP + k, d]
+                rows[k * 128 + d : k * 128 + d + 1, :] = table[pl.ds(place, 1), :]
+        for k in range(GROUP):
+            r = step * GROUP + k
             both = rows[k * 128 : k * 128 + 128, :].T
             upper = half_ref[pl.ds(r, 1), :] > 0
             turned[pl.ds(pl.multiple_of(r * 64, 64), 64), :] = jnp.where(upper, both[64:], both[:64])
         return 0
 
-    lax.fori_loop(0, SLOTS // 2, pair, 0)
+    lax.fori_loop(0, SLOTS // GROUP, some, 0)
 
 
 def split_index(sends_ref, row_ref, half_ref):
-    turned = sends_ref[...].T
+    turned = sends_ref[...]
     half_ref[...] = turned // HALF
     row_ref[...] = turned % HALF
 
@@ -202,22 +207,32 @@
 
 
 def entries_in_order(got, hot, slots, split, entry):
+    zero = jnp.zeros((32, LANES), BF16)
+    fine = {0: 288, 1: 320, 5: 352}
     for g, size in ((0, 128), (1, 128), (2, 32)):
-        parts = split3(got[:, 0, g * 128 : g * 128 + 128].T[0:size])
-        for k in range(3):
-            split[g * 128 : g * 128 + size, k * 128 : k * 128 + 128] = parts[k]
+        high, mid, low = split3(got[:, 0, g * 128 : g * 128 + 128].T[0:size])
+        split[g * 128 : g * 128 + size, 0:128] = high
+        split[g * 128 : g * 128 + size, 128:256] = mid
+        for v, row in fine.items():
+            if v // 4 == g:
+                first = (v - g * 4) * 32
+                split[row : row + 32, 0:128] = low[first : first + 32]
+                split[row : row + 32, 128:256] = zero
     rows = iota((SLOTS, LANES), 0)
 
     def step(q, _):
         cols = hot[:, pl.ds(pl.multiple_of(q * LANES, LANES), LANES)]
-        picked = dot_nn(split[...], jnp.concatenate([cols, cols, cols], 0))
+        picked = dot_nn(split[...], jnp.concatenate([cols, cols], 0))
         here = rows == slots[pl.ds(q, 1), :] % SLOTS
         for v in range(9):
-            kept = jnp.where(here, picked[v * 32 : v * 32 + 32], 0.0)
+            value = picked[v * 32 : v * 32 + 32]
+            if v in fine:
+                value = value + picked[fine[v] : fine[v] + 32]
+            kept = jnp.where(here, value, 0.0)
             entry[pl.ds(v * 32 + q, 1), :] = jnp.sum(kept, axis=0, keepdims=True)
         return 0
 
-    lax.fori_loop(0, STEPS, step, 0, unroll=2)
+    lax.fori_loop(0, STEPS, step, 0, unroll=UNROLL_ENTRY)
 
 
 def power_factors(entry, counts, factor):
@@ -258,7 +273,7 @@
         shade[pl.ds(first, LANES), :] = out[:, 256:640]
         return 0
 
-    lax.fori_loop(0, STEPS, step, 0, unroll=2)
+    lax.fori_loop(0, STEPS, step, 0, unroll=UNROLL_ALPHA)
 
 
 def composite(alpha, shade, image):
@@ -300,7 +315,7 @@
     lax.fori_loop(0, STEPS, step, (one, one))
 
 
-def backward(alpha, shade, weights, cot, pull, held):
+def backward(alpha, shade, weights, cot, parts):
     up = [cot[ch, :, h * 128 : h * 128 + 128] for ch in range(3) for h in range(2)]
     zero = jnp.zeros((16, LANES), F32)
 
@@ -317,38 +332,39 @@
                 ahead = value - behind[h]
                 behind[h] = behind[h] + opaque * ahead
                 pulled = jnp.where(opaque < 0.99, weight * ahead, 0.0)
-                high, low = split2(pulled)
-                pull[row, h * 128 : h * 128 + 128] = high
-                pull[row, 256 + h * 128 : 384 + h * 128] = low
-                high, low = split2(weight)
-                held[row, h * 128 : h * 128 + 128] = high
-                held[row, 256 + h * 128 : 384 + h * 128] = low
+                pieces = split2(pulled) + split2(weight)
+                for p, piece in enumerate(pieces):
+                    parts[row, p * 256 + h * 128 : p * 256 + h * 128 + 128] = piece
         return tuple(behind)
 
     lax.fori_loop(0, STEPS, step, (zero, zero))
 
 
-def pixel_sums(pull, held, moments, cot, cots, sums):
-    flat = cot[...].reshape(48, 256)
-    high, low = split2(flat)
-    cots[:, 0:256] = high
-    cots[:, 256:512] = high
-    cots[:, 512:768] = low
+def pixel_sums(parts, moments, cot, against, sums):
+    high, low = split2(cot[...].reshape(48, 256))
+    against[...] = jnp.zeros((LANES, 1024), BF16)
+    against[0:16, 0:512] = moments[...]
+    against[16:64, 512:768] = high
+    against[16:64, 768:1024] = high
+    against[64:112, 512:768] = low
     own = iota((16, LANES), 0) == iota((16, LANES), 1) % 16
 
-    def step(q, _):
-        row = pl.ds(pl.multiple_of(q * LANES, LANES), LANES)
-        moment = dot_nt(moments[...], pull[row, :])
-        for v in range(6):
-            sums[pl.ds(v * 32 + q, 1), :] = moment[v : v + 1]
-        both = held[row, :]
-        spread = dot_nt(cots[...], jnp.concatenate([both, both[:, 0:256]], 1))
-        for ch in range(3):
-            kept = jnp.where(own, spread[ch * 16 : ch * 16 + 16], 0.0)
-            sums[pl.ds((6 + ch) * 32 + q, 1), :] = jnp.sum(kept, axis=0, keepdims=True)
-        return 0
-
-    lax.fori_loop(0, STEPS, step, 0, unroll=2)
+    def step(s, _):
+        row = pl.ds(pl.multiple_of(s * 1024, 1024), 1024)
+        totals = dot_nt(parts[row, :], against[...])
+        for k in range(8):
+            q = s * 8 + k
+            turned = totals[k * 128 : k * 128 + 128].T
+            for v in range(6):
+                sums[pl.ds(v * 32 + q, 1), :] = turned[v : v + 1]
+            for ch in range(3):
+                first = 16 + ch * 16
+                value = turned[first : first + 16] + turned[first + 48 : first + 64]
+                kept = jnp.where(own, value, 0.0)
+                sums[pl.ds((6 + ch) * 32 + q, 1), :] = jnp.sum(kept, axis=0, keepdims=True)
+        return 0
+
+    lax.fori_loop(0, STEPS // 8, step, 0)
 
 
 def entry_gradients(entry, sums, grad):
@@ -412,7 +428,7 @@
         pl.semaphore_signal(barrier, inc=1, device_id=place_of(lax.rem(me + k, N_DEV)), device_id_type=MESH)
         return 0
 
-    lax.fori_loop(1, N_DEV, one, 0)
+    lax.fori_loop(1, N_DEV, one, 0, unroll=8)
 
 
 def await_greetings():
@@ -432,7 +448,7 @@
         ).start()
         return 0
 
-    lax.fori_loop(1, N_DEV, one, 0)
+    lax.fori_loop(1, N_DEV, one, 0, unroll=8)
     got[me] = msg[me]
 
 
@@ -454,7 +470,7 @@
     ask, asked, msg_cur, got_cur, msg_next, got_next, back, got_back,
     slots_next, slots_cur, hot_next, hot_cur, turned, mark,
     held_params, table, rows, rows_cur, rows_next, row_v, half_next, half_cur, row_next, row_cur, basis_next, color,
-    split, entry, factor, alpha, shade, weights, pull, held, cots, sums, grad, spread,
+    split, entry, factor, alpha, shade, weights, parts, against, sums, grad, spread,
     send_sems, recv_sems, param_sems, index_sems,
 ):
     me = lax.axis_index("gauss") * N_PIX + lax.axis_index("pix")
@@ -477,15 +493,15 @@
     owner_onehot(slots_cur, hot_cur)
     tiles_cur = slot_tiles(slots_cur, hot_cur, mark)
     ask[:, 0, :] = angle_message(tiles_next, tiles_cur, angles_next, angles_cur)
+    for copy in to_smem:
+        copy.wait()
+    build_table(copies, held_params, table)
     await_greetings()
     links = [
         (me, src, dst, send_sems.at[k], recv_sems.at[k])
         for k, (src, dst) in enumerate(((ask, asked), (msg_cur, got_cur), (msg_next, got_next), (back, got_back)))
     ]
     send_all(*links[0])
-    for copy in to_smem:
-        copy.wait()
-    build_table(copies, held_params, table)
     gather_rows(row_cur, table, rows, half_cur, rows_cur)
     all_of(*links[0]).wait_recv()
     seen = asked[:, 0, :].T
@@ -506,8 +522,8 @@
     power_factors(entry, counts_cur, factor)
     alphas_and_colors(factor, power, alpha, shade)
     weights_forward(alpha, weights)
-    backward(alpha, shade, weights, cot, pull, held)
-    pixel_sums(pull, held, moments, cot, cots, sums)
+    backward(alpha, shade, weights, cot, parts)
+    pixel_sums(parts, moments, cot, against, sums)
     entry_gradients(entry, sums, grad)
     slots_in_order(grad, hot_cur, slots_cur, spread, back)
     back[:, 0, 288:384] = jnp.zeros((N_DEV, 96), F32)
@@ -524,49 +540,69 @@
         all_of(*link).wait_send()
 
 
-def scatter_kernel(turned, basis, sends, grads, row_v, half, row_s, total, piece, rows, sem):
+def scatter_kernel(turned, basis, sends, grads, row_v, half, row_s, total, piece, rows, out, sem, out_sems):
     split_index(sends, row_v, half)
     copy = pltpu.make_async_copy(row_v, row_s, sem)
     copy.start()
 
     def clear(b, _):
-        total[pl.ds(pl.multiple_of(b * 256, 256), 256), :] = jnp.zeros((256, LANES), F32)
-        return 0
-
-    lax.fori_loop(0, HALF // 256, clear, 0)
-    piece[48:64, :] = jnp.zeros((16, LANES), F32)
+        total[pl.ds(pl.multiple_of(b * 512, 512), 512), :] = jnp.zeros((512, LANES), F32)
+        return 0
+
+    piece[...] = jnp.zeros((2, 64, LANES), F32)
     same_group = iota((LANES, LANES), 0) // 16 == iota((LANES, LANES), 1) // 16
-    copy.wait()
-
-    def slot(r, _):
-        piece[0:6, :] = turned[pl.ds(r, 8, stride=32), :][0:6]
+
+    def prepare(r, k):
+        piece[k, 0:6, :] = turned[pl.ds(r, 8, stride=32), :][0:6]
         terms = basis[pl.ds(r, 16, stride=32), :]
         for ch in range(3):
-            piece[6 + 16 * ch : 22 + 16 * ch, :] = terms * turned[pl.ds((6 + ch) * 32 + r, 1), :]
+            piece[k, 6 + 16 * ch : 22 + 16 * ch, :] = terms * turned[pl.ds((6 + ch) * 32 + r, 1), :]
         upper = half[pl.ds(r, 1), :] > 0
-        values = piece[...]
+        values = piece[k]
         both = jnp.concatenate([jnp.where(upper, 0.0, values), jnp.where(upper, values, 0.0)], 0)
         high, low = split2(both)
         name = jnp.broadcast_to(row_v[pl.ds(r, 1), :].astype(F32), (LANES, LANES))
         same = jnp.logical_and(name == name.T, same_group).astype(F32).astype(BF16)
-        rows[...] = dot_nt(jnp.concatenate([same, same], 1), jnp.concatenate([high, low], 1))
+        rows[k] = dot_nt(jnp.concatenate([same, same], 1), jnp.concatenate([high, low], 1))
+
+    def add(r, k):
         for g in range(8):
             places = [row_s[r, g * 16 + u] for u in range(16)]
             olds = [total[pl.ds(places[u], 1), :] for u in range(16)]
             for u in range(16):
-                total[pl.ds(places[u], 1), :] = olds[u] + rows[g * 16 + u : g * 16 + u + 1, :]
-        return 0
-
-    lax.fori_loop(0, SLOTS, slot, 0)
-
-    def block(b, _):
-        first = pl.multiple_of(b * LANES, LANES)
-        both = total[pl.ds(first, LANES), :].T
-        grads[:, pl.ds(first, LANES)] = both[0:ROWS]
-        grads[:, pl.ds(first + HALF, LANES)] = both[64 : 64 + ROWS]
-        return 0
-
-    lax.fori_loop(0, HALF // LANES, block, 0, unroll=4)
+                total[pl.ds(places[u], 1), :] = olds[u] + rows[k, g * 16 + u : g * 16 + u + 1, :]
+
+    prepare(0, 0)
+    lax.fori_loop(0, HALF // 512, clear, 0)
+    copy.wait()
+
+    def slots(s, _):
+        prepare(s * 2 + 1, 1)
+        add(s * 2, 0)
+        prepare(lax.rem(s * 2 + 2, SLOTS), 0)
+        add(s * 2 + 1, 1)
+        return 0
+
+    lax.fori_loop(0, SLOTS // 2, slots, 0)
+
+    width = HALF // CHUNKS
+    writes = []
+    for c in range(CHUNKS):
+        def block(b, _):
+            first = pl.multiple_of(c * width + b * LANES, LANES)
+            both = total[pl.ds(first, LANES), :].T
+            out[:, pl.ds(first, LANES)] = both[0:ROWS]
+            out[:, pl.ds(first + HALF, LANES)] = both[64 : 64 + ROWS]
+            return 0
+
+        lax.fori_loop(0, width // LANES, block, 0, unroll=8)
+        for k in range(2):
+            cols = pl.ds(k * HALF + c * width, width)
+            write = pltpu.make_async_copy(out.at[:, cols], grads.at[:, cols], out_sems.at[c * 2 + k])
+            write.start()
+            writes.append(write)
+    for write in writes:
+        write.wait()
 
 
 VM = pl.BlockSpec(memory_space=pltpu.VMEM)
@@ -599,7 +635,7 @@
             pltpu.VMEM((SLOTS, 4096), BF16),
             pltpu.VMEM((ROWS, GAUSS), F32),
             pltpu.VMEM((HALF, LANES), F32),
-            pltpu.VMEM((256, LANES), F32),
+            pltpu.VMEM((GROUP * LANES, LANES), F32),
             pltpu.VMEM((SLOTS * 64 + 8, LANES), F32),
             pltpu.VMEM((SLOTS * 64 + 8, LANES), F32),
             pltpu.VMEM((2,) + dense, I32),
@@ -609,15 +645,14 @@
             pltpu.SMEM(dense, I32),
             pltpu.VMEM((544, LANES), F32),
             pltpu.VMEM((96, LANES), F32),
-            pltpu.VMEM((288, 384), BF16),
+            pltpu.VMEM((384, 256), BF16),
             pltpu.VMEM((288, LANES), F32),
             pltpu.VMEM((1056, LANES), F32),
             pltpu.VMEM((4096, 256), F32),
             pltpu.VMEM((4096, 384), F32),
             pltpu.VMEM((4096, 256), F32),
-            pltpu.VMEM((4096, 512), BF16),
-            pltpu.VMEM((4096, 512), BF16),
-            pltpu.VMEM((48, 768), BF16),
+            pltpu.VMEM((4096, 1024), BF16),
+            pltpu.VMEM((LANES, 1024), BF16),
             pltpu.VMEM((288, LANES), F32),
             pltpu.VMEM((288, LANES), F32),
             pltpu.VMEM((576, 4096), BF16),
@@ -630,25 +665,27 @@
             vmem_limit_bytes=VMEM_LIMIT, collective_id=0, has_side_effects=True
         ),
         name="main",
-    )(params, lists_next, lists_cur, angles_next, angles_cur, counts_next, counts_cur,
-      sends_next[0], sends_cur[0], jnp.transpose(cotangent, (1, 0, 2)), power, moments)
+    )(params, lists_next, lists_cur, jnp.transpose(angles_next), jnp.transpose(angles_cur), counts_next, counts_cur,
+      jnp.transpose(sends_next[0]), jnp.transpose(sends_cur[0]), jnp.transpose(cotangent, (1, 0, 2)), power, moments)
     grads = pl.pallas_call(
         scatter_kernel,
         out_shape=shape((ROWS, GAUSS)),
         in_specs=[VM] * 3,
-        out_specs=VM,
+        out_specs=pl.BlockSpec(memory_space=pl.ANY),
         scratch_shapes=[
             pltpu.VMEM(dense, I32),
             pltpu.VMEM(dense, I32),
             pltpu.SMEM(dense, I32),
             pltpu.VMEM((HALF, LANES), F32),
-            pltpu.VMEM((64, LANES), F32),
-            pltpu.VMEM((LANES, LANES), F32),
+            pltpu.VMEM((2, 64, LANES), F32),
+            pltpu.VMEM((2, LANES, LANES), F32),
+            pltpu.VMEM((ROWS, GAUSS), F32),
             pltpu.SemaphoreType.DMA,
+            pltpu.SemaphoreType.DMA((2 * CHUNKS,)),
         ],
         compiler_params=PARAMS,
         name="scatter",
-    )(returned, basis, sends_cur[0])
+    )(returned, basis, jnp.transpose(sends_cur[0]))
     return jnp.transpose(image, (1, 0, 2)), grads
 
 

time: 95.7 us -> 65.4 us (0.68)
  Pallas kernels: 88.5 us -> 64 us
  local copies, waits for them, and re-layouts: 6.21 us -> 0.63 us
    pallas_call x1, Pallas kernels: 71.6 us -> 53.6 us  [body(): pl.pallas_call(main_kernel, out_shape=(shape((3, 16, 256)), shape((384, L...]
    pallas_call x1, Pallas kernels: 16.9 us -> 10.4 us  [body(): pl.pallas_call(scatter_kernel, out_shape=shape((ROWS, GAUSS)), in_specs=[...]
    unnamed x7 -> x3, local copies, waits for them, and re-layouts: 6.21 us -> 0.63 us
where the time goes in v2:
time: 65.4 us; the launch traced here: 65.3 us
  Pallas kernels  64 us (98%)
  between operations  0.66 us (1%)
    pallas_call x1, Pallas kernels, body(): pl.pallas_call(main_kernel, out_shape=(shape((3, 16, 256)), shape((384, L...  53.6 us
    pallas_call x1, Pallas kernels, body(): pl.pallas_call(scatter_kernel, out_shape=shape((ROWS, GAUSS)), in_specs=[...  10.4 us

profile of v2, /device:TPU:1, one launch (start us, length us, event | category | flops | bytes accessed | tf_op | source)
XLA Modules:
  0.0 65.3 jit_solution(14488569855741656264)
XLA Ops:
  0.6 53.6 %main.1 = (f32[3,16,256]{2,1,0:T(8,128)}, f32[384,128]{1,0:T(8,128)}, f32[544,128]{1,0:T(8,128)}) custom-call(f32[54,16384]{1,0:T(8,128)} %params.1, s32[16,256]{1,0:T(8,128)} %lists_next.1, s32[16,256]{1,0:T(8,128)} %lists_cur.1, f32[2,16]{1,0:T(2,128)} %bitcast.15, f32[2,16]{1,0:T(2,128)} %bitcast.16, s32[16]{0:T(128)} %counts_next.1, s32[16]{0:T(128)} %counts_cur.1, ...), custom_call_target="tpu_custom_call" | custom-call | tf_op jit(solution)/shard_map/main/pallas_call | solution.py:621
  54.2 0.0 copy-start
  54.2 10.4 %scatter.1 = f32[54,16384]{1,0:T(8,128)} custom-call(f32[384,128]{1,0:T(8,128)} %get-tuple-element.6.turned, f32[544,128]{1,0:T(8,128)} %get-tuple-element.7.basis, s32[32,128]{1,0:T(8,128)} %bitcast.11), custom_call_target="tpu_custom_call" | custom-call | tf_op jit(solution)/shard_map/scatter/pallas_call | solution.py:670
  64.6 0.0 copy-done
  64.6 0.6 copy.15
Async XLA Ops:
  54.2 10.4 %copy-start = (f32[3,16,256]{2,1,0:T(8,128)S(1)}, f32[3,16,256]{2,1,0:T(8,128)}, u32[]{:S(2)}) copy-start(f32[3,16,256]{2,1,0:T(8,128)} %get-tuple-element.5) | copy-start | bytes 147460

commit v3 on v2

--- a/solution.py
+++ b/solution.py
@@ -17,6 +17,9 @@
 HALF = 8192
 CHUNKS = 4
 UNROLL_ENTRY = 8
+BACK = 4
+PAIR = 8
+WIDE = 2
 UNROLL_ALPHA = 8
 GROUP = 8
 ROWS = 54
@@ -220,19 +223,22 @@
                 split[row : row + 32, 128:256] = zero
     rows = iota((SLOTS, LANES), 0)
 
-    def step(q, _):
-        cols = hot[:, pl.ds(pl.multiple_of(q * LANES, LANES), LANES)]
+    def step(s, _):
+        cols = hot[:, pl.ds(pl.multiple_of(s * WIDE * LANES, WIDE * LANES), WIDE * LANES)]
         picked = dot_nn(split[...], jnp.concatenate([cols, cols], 0))
-        here = rows == slots[pl.ds(q, 1), :] % SLOTS
-        for v in range(9):
-            value = picked[v * 32 : v * 32 + 32]
-            if v in fine:
-                value = value + picked[fine[v] : fine[v] + 32]
-            kept = jnp.where(here, value, 0.0)
-            entry[pl.ds(v * 32 + q, 1), :] = jnp.sum(kept, axis=0, keepdims=True)
-        return 0
-
-    lax.fori_loop(0, STEPS, step, 0, unroll=UNROLL_ENTRY)
+        for k in range(WIDE):
+            q = s * WIDE + k
+            lane = slice(k * LANES, k * LANES + LANES)
+            here = rows == slots[pl.ds(q, 1), :] % SLOTS
+            for v in range(9):
+                value = picked[v * 32 : v * 32 + 32, lane]
+                if v in fine:
+                    value = value + picked[fine[v] : fine[v] + 32, lane]
+                kept = jnp.where(here, value, 0.0)
+                entry[pl.ds(v * 32 + q, 1), :] = jnp.sum(kept, axis=0, keepdims=True)
+        return 0
+
+    lax.fori_loop(0, STEPS // WIDE, step, 0, unroll=UNROLL_ENTRY // WIDE)
 
 
 def power_factors(entry, counts, factor):
@@ -315,15 +321,22 @@
     lax.fori_loop(0, STEPS, step, (one, one))
 
 
-def backward(alpha, shade, weights, cot, parts):
+def backward(alpha, shade, weights, cot, moments, parts, parts_odd, against, sums):
     up = [cot[ch, :, h * 128 : h * 128 + 128] for ch in range(3) for h in range(2)]
     zero = jnp.zeros((16, LANES), F32)
-
-    def step(s, behind):
+    high, low = split2(cot[...].reshape(48, 256))
+    against[...] = jnp.zeros((LANES, 1024), BF16)
+    against[0:16, 0:512] = moments[...]
+    against[16:64, 512:768] = high
+    against[16:64, 768:1024] = high
+    against[64:112, 512:768] = low
+    own = iota((16, LANES), 0) == iota((16, LANES), 1) % 16
+
+    def pull(s, behind, parts):
         behind = list(behind)
-        q = STEPS - 1 - s
-        for k in range(7, -1, -1):
-            row = pl.ds(pl.multiple_of(q * LANES + k * 16, 16), 16)
+        for k in range(8 * BACK - 1, -1, -1):
+            row = pl.ds(pl.multiple_of(s * BACK * LANES + k * 16, 16), 16)
+            local = slice(k * 16, k * 16 + 16)
             colors = [shade[row, ch * 128 : ch * 128 + 128] for ch in range(3)]
             for h in range(2):
                 opaque = alpha[row, h * 128 : h * 128 + 128]
@@ -334,26 +347,13 @@
                 pulled = jnp.where(opaque < 0.99, weight * ahead, 0.0)
                 pieces = split2(pulled) + split2(weight)
                 for p, piece in enumerate(pieces):
-                    parts[row, p * 256 + h * 128 : p * 256 + h * 128 + 128] = piece
+                    parts[local, p * 256 + h * 128 : p * 256 + h * 128 + 128] = piece
         return tuple(behind)
 
-    lax.fori_loop(0, STEPS, step, (zero, zero))
-
-
-def pixel_sums(parts, moments, cot, against, sums):
-    high, low = split2(cot[...].reshape(48, 256))
-    against[...] = jnp.zeros((LANES, 1024), BF16)
-    against[0:16, 0:512] = moments[...]
-    against[16:64, 512:768] = high
-    against[16:64, 768:1024] = high
-    against[64:112, 512:768] = low
-    own = iota((16, LANES), 0) == iota((16, LANES), 1) % 16
-
-    def step(s, _):
-        row = pl.ds(pl.multiple_of(s * 1024, 1024), 1024)
-        totals = dot_nt(parts[row, :], against[...])
-        for k in range(8):
-            q = s * 8 + k
+    def add_up(s, parts):
+        totals = dot_nt(parts[...], against[...])
+        for k in range(BACK):
+            q = s * BACK + k
             turned = totals[k * 128 : k * 128 + 128].T
             for v in range(6):
                 sums[pl.ds(v * 32 + q, 1), :] = turned[v : v + 1]
@@ -362,9 +362,21 @@
                 value = turned[first : first + 16] + turned[first + 48 : first + 64]
                 kept = jnp.where(own, value, 0.0)
                 sums[pl.ds((6 + ch) * 32 + q, 1), :] = jnp.sum(kept, axis=0, keepdims=True)
-        return 0
-
-    lax.fori_loop(0, STEPS // 8, step, 0)
+
+    last = STEPS // BACK - 1
+
+    def step(j, behind):
+        s = last - 1 - 2 * j
+        behind = pull(s, behind, parts_odd)
+        add_up(s + 1, parts)
+        behind = pull(s - 1, behind, parts)
+        add_up(s, parts_odd)
+        return behind
+
+    behind = lax.fori_loop(0, STEPS // BACK // 2 - 1, step, pull(last, (zero, zero), parts))
+    pull(0, behind, parts_odd)
+    add_up(1, parts)
+    add_up(0, parts_odd)
 
 
 def entry_gradients(entry, sums, grad):
@@ -411,10 +423,12 @@
         return 0
 
     lax.fori_loop(0, STEPS, step, 0, unroll=2)
-    for g, size in ((0, 128), (1, 128), (2, 32)):
-        high = dot_nt(hot[...], spread[g * 128 : g * 128 + size, :])
-        low = dot_nt(hot[...], spread[288 + g * 128 : 288 + g * 128 + size, :])
-        msg[:, 0, g * 128 : g * 128 + size] = high + low
+    both = dot_nt(spread[...], hot[...])
+    total = both[0:288] + both[288:576]
+    msg[:, 0, 0:128] = total[0:128].T
+    msg[:, 0, 128:256] = total[128:256].T
+    last = total[256:288]
+    msg[:, 0, 256:384] = jnp.concatenate([last, last, last, last], 0).T
 
 
 def place_of(device):
@@ -428,7 +442,7 @@
         pl.semaphore_signal(barrier, inc=1, device_id=place_of(lax.rem(me + k, N_DEV)), device_id_type=MESH)
         return 0
 
-    lax.fori_loop(1, N_DEV, one, 0, unroll=8)
+    lax.fori_loop(1, N_DEV, one, 0, unroll=N_DEV - 1)
 
 
 def await_greetings():
@@ -448,7 +462,7 @@
         ).start()
         return 0
 
-    lax.fori_loop(1, N_DEV, one, 0, unroll=8)
+    lax.fori_loop(1, N_DEV, one, 0, unroll=N_DEV - 1)
     got[me] = msg[me]
 
 
@@ -470,7 +484,7 @@
     ask, asked, msg_cur, got_cur, msg_next, got_next, back, got_back,
     slots_next, slots_cur, hot_next, hot_cur, turned, mark,
     held_params, table, rows, rows_cur, rows_next, row_v, half_next, half_cur, row_next, row_cur, basis_next, color,
-    split, entry, factor, alpha, shade, weights, parts, against, sums, grad, spread,
+    split, entry, factor, alpha, shade, weights, parts, parts_odd, against, sums, grad, spread,
     send_sems, recv_sems, param_sems, index_sems,
 ):
     me = lax.axis_index("gauss") * N_PIX + lax.axis_index("pix")
@@ -522,11 +536,9 @@
     power_factors(entry, counts_cur, factor)
     alphas_and_colors(factor, power, alpha, shade)
     weights_forward(alpha, weights)
-    backward(alpha, shade, weights, cot, parts)
-    pixel_sums(parts, moments, cot, against, sums)
+    backward(alpha, shade, weights, cot, moments, parts, parts_odd, against, sums)
     entry_gradients(entry, sums, grad)
     slots_in_order(grad, hot_cur, slots_cur, spread, back)
-    back[:, 0, 288:384] = jnp.zeros((N_DEV, 96), F32)
     send_all(*links[3])
     all_of(*links[2]).wait_recv()
     entries_in_order(got_next, hot_next, slots_next, split, entry)
@@ -577,13 +589,12 @@
     copy.wait()
 
     def slots(s, _):
-        prepare(s * 2 + 1, 1)
-        add(s * 2, 0)
-        prepare(lax.rem(s * 2 + 2, SLOTS), 0)
-        add(s * 2 + 1, 1)
-        return 0
-
-    lax.fori_loop(0, SLOTS // 2, slots, 0)
+        for k in range(PAIR):
+            prepare(lax.rem(s * PAIR + k + 1, SLOTS), (k + 1) % 2)
+            add(s * PAIR + k, k % 2)
+        return 0
+
+    lax.fori_loop(0, SLOTS // PAIR, slots, 0)
 
     width = HALF // CHUNKS
     writes = []
@@ -651,7 +662,8 @@
             pltpu.VMEM((4096, 256), F32),
             pltpu.VMEM((4096, 384), F32),
             pltpu.VMEM((4096, 256), F32),
-            pltpu.VMEM((4096, 1024), BF16),
+            pltpu.VMEM((BACK * LANES, 1024), BF16),
+            pltpu.VMEM((BACK * LANES, 1024), BF16),
             pltpu.VMEM((LANES, 1024), BF16),
             pltpu.VMEM((288, LANES), F32),
             pltpu.VMEM((288, LANES), F32),

time: 65.4 us -> 60.2 us (0.920)
  Pallas kernels: 64 us -> 58.7 us
    pallas_call x1, Pallas kernels: 53.6 us -> 48.6 us  [body(): pl.pallas_call(main_kernel, out_shape=(shape((3, 16, 256)), shape((384, L...]
where the time goes in v3:
time: 60.2 us; the launch traced here: 60 us
  Pallas kernels  58.7 us (98%)
  between operations  0.67 us (1%)
  local copies, waits for them, and re-layouts  0.63 us (1%)
    pallas_call x1, Pallas kernels, body(): pl.pallas_call(main_kernel, out_shape=(shape((3, 16, 256)), shape((384, L...  48.6 us
    pallas_call x1, Pallas kernels, body(): pl.pallas_call(scatter_kernel, out_shape=shape((ROWS, GAUSS)), in_specs=[...  10.1 us

profile of v3, /device:TPU:1, one launch (start us, length us, event | category | flops | bytes accessed | tf_op | source)
XLA Modules:
  0.0 60.0 jit_solution(9890270973789063018)
XLA Ops:
  0.6 48.6 %main.1 = (f32[3,16,256]{2,1,0:T(8,128)}, f32[384,128]{1,0:T(8,128)}, f32[544,128]{1,0:T(8,128)}) custom-call(f32[54,16384]{1,0:T(8,128)} %params.1, s32[16,256]{1,0:T(8,128)} %lists_next.1, s32[16,256]{1,0:T(8,128)} %lists_cur.1, f32[2,16]{1,0:T(2,128)} %bitcast.15, f32[2,16]{1,0:T(2,128)} %bitcast.16, s32[16]{0:T(128)} %counts_next.1, s32[16]{0:T(128)} %counts_cur.1, ...), custom_call_target="tpu_custom_call" | custom-call | tf_op jit(solution)/shard_map/main/pallas_call | solution.py:632
  49.3 0.0 copy-start
  49.3 10.1 %scatter.1 = f32[54,16384]{1,0:T(8,128)} custom-call(f32[384,128]{1,0:T(8,128)} %get-tuple-element.6.turned, f32[544,128]{1,0:T(8,128)} %get-tuple-element.7.basis, s32[32,128]{1,0:T(8,128)} %bitcast.11), custom_call_target="tpu_custom_call" | custom-call | tf_op jit(solution)/shard_map/scatter/pallas_call | solution.py:682
  59.4 0.0 copy-done
  59.4 0.6 %copy.15 = f32[16,3,256]{2,0,1:T(8,128)} copy(f32[16,3,256]{2,0,1:T(8,128)S(1)} %bitcast.13) | data formatting | bytes 98304
Async XLA Ops:
  49.3 10.1 %copy-start = (f32[3,16,256]{2,1,0:T(8,128)S(1)}, f32[3,16,256]{2,1,0:T(8,128)}, u32[]{:S(2)}) copy-start(f32[3,16,256]{2,1,0:T(8,128)} %get-tuple-element.5) | copy-start | bytes 147460

commit v4 on v3

--- a/solution.py
+++ b/solution.py
@@ -409,25 +409,40 @@
         grad[v * 32 : v * 32 + 32, :] = value
 
 
-def slots_in_order(grad, hot, slots, spread, msg):
+def slots_in_order(grad, hot, slots, spread, spread_odd, folded, msg):
     rows = iota((SLOTS, LANES), 0)
 
-    def step(q, _):
-        first = pl.multiple_of(q * LANES, LANES)
-        here = rows == slots[pl.ds(q, 1), :] % SLOTS
-        for v in range(9):
-            value = grad[pl.ds(v * 32 + q, 1), :]
-            high, low = split2(jnp.where(here, value, 0.0))
-            spread[v * 32 : v * 32 + 32, pl.ds(first, LANES)] = high
-            spread[288 + v * 32 : 320 + v * 32, pl.ds(first, LANES)] = low
-        return 0
-
-    lax.fori_loop(0, STEPS, step, 0, unroll=2)
-    both = dot_nt(spread[...], hot[...])
-    total = both[0:288] + both[288:576]
-    msg[:, 0, 0:128] = total[0:128].T
-    msg[:, 0, 128:256] = total[128:256].T
-    last = total[256:288]
+    def build(c, buffer):
+        for k in range(4):
+            q = c * 4 + k
+            lane = slice(k * LANES, k * LANES + LANES)
+            here = rows == slots[pl.ds(q, 1), :] % SLOTS
+            for v in range(9):
+                value = grad[pl.ds(v * 32 + q, 1), :]
+                high, low = split2(jnp.where(here, value, 0.0))
+                buffer[v * 32 : v * 32 + 32, lane] = high
+                buffer[288 + v * 32 : 320 + v * 32, lane] = low
+
+    def fold(c, buffer):
+        both = dot_nt(buffer[...], hot[:, pl.ds(pl.multiple_of(c * 512, 512), 512)])
+        folded[...] += both[0:288] + both[288:576]
+
+    def step(j, _):
+        build(2 * j + 1, spread_odd)
+        fold(2 * j, spread)
+        build(2 * j + 2, spread)
+        fold(2 * j + 1, spread_odd)
+        return 0
+
+    folded[...] = jnp.zeros((288, LANES), F32)
+    build(0, spread)
+    lax.fori_loop(0, STEPS // 8 - 1, step, 0)
+    build(STEPS // 4 - 1, spread_odd)
+    fold(STEPS // 4 - 2, spread)
+    fold(STEPS // 4 - 1, spread_odd)
+    msg[:, 0, 0:128] = folded[0:128, :].T
+    msg[:, 0, 128:256] = folded[128:256, :].T
+    last = folded[256:288, :]
     msg[:, 0, 256:384] = jnp.concatenate([last, last, last, last], 0).T
 
 
@@ -484,7 +499,7 @@
     ask, asked, msg_cur, got_cur, msg_next, got_next, back, got_back,
     slots_next, slots_cur, hot_next, hot_cur, turned, mark,
     held_params, table, rows, rows_cur, rows_next, row_v, half_next, half_cur, row_next, row_cur, basis_next, color,
-    split, entry, factor, alpha, shade, weights, parts, parts_odd, against, sums, grad, spread,
+    split, entry, factor, alpha, shade, weights, parts, parts_odd, against, sums, grad, spread, spread_odd, folded,
     send_sems, recv_sems, param_sems, index_sems,
 ):
     me = lax.axis_index("gauss") * N_PIX + lax.axis_index("pix")
@@ -538,7 +553,7 @@
     weights_forward(alpha, weights)
     backward(alpha, shade, weights, cot, moments, parts, parts_odd, against, sums)
     entry_gradients(entry, sums, grad)
-    slots_in_order(grad, hot_cur, slots_cur, spread, back)
+    slots_in_order(grad, hot_cur, slots_cur, spread, spread_odd, folded, back)
     send_all(*links[3])
     all_of(*links[2]).wait_recv()
     entries_in_order(got_next, hot_next, slots_next, split, entry)
@@ -552,7 +567,9 @@
         all_of(*link).wait_send()
 
 
-def scatter_kernel(turned, basis, sends, grads, row_v, half, row_s, total, piece, rows, out, sem, out_sems):
+def scatter_kernel(turned, basis, sends, drawn, grads, image, row_v, half, row_s, total, piece, rows, out, sem, image_sem, out_sems):
+    handed = pltpu.make_async_copy(drawn, image, image_sem)
+    handed.start()
     split_index(sends, row_v, half)
     copy = pltpu.make_async_copy(row_v, row_s, sem)
     copy.start()
@@ -614,6 +631,7 @@
             writes.append(write)
     for write in writes:
         write.wait()
+    handed.wait()
 
 
 VM = pl.BlockSpec(memory_space=pltpu.VMEM)
@@ -667,7 +685,9 @@
             pltpu.VMEM((LANES, 1024), BF16),
             pltpu.VMEM((288, LANES), F32),
             pltpu.VMEM((288, LANES), F32),
-            pltpu.VMEM((576, 4096), BF16),
+            pltpu.VMEM((576, 512), BF16),
+            pltpu.VMEM((576, 512), BF16),
+            pltpu.VMEM((288, LANES), F32),
             pltpu.SemaphoreType.DMA((4,)),
             pltpu.SemaphoreType.DMA((4,)),
             pltpu.SemaphoreType.DMA((2 * CHUNKS,)),
@@ -679,11 +699,11 @@
         name="main",
     )(params, lists_next, lists_cur, jnp.transpose(angles_next), jnp.transpose(angles_cur), counts_next, counts_cur,
       jnp.transpose(sends_next[0]), jnp.transpose(sends_cur[0]), jnp.transpose(cotangent, (1, 0, 2)), power, moments)
-    grads = pl.pallas_call(
+    grads, image = pl.pallas_call(
         scatter_kernel,
-        out_shape=shape((ROWS, GAUSS)),
-        in_specs=[VM] * 3,
-        out_specs=pl.BlockSpec(memory_space=pl.ANY),
+        out_shape=(shape((ROWS, GAUSS)), shape((3, 16, 256))),
+        in_specs=[VM] * 3 + [pl.BlockSpec(memory_space=pl.ANY)],
+        out_specs=(pl.BlockSpec(memory_space=pl.ANY),) * 2,
         scratch_shapes=[
             pltpu.VMEM(dense, I32),
             pltpu.VMEM(dense, I32),
@@ -693,11 +713,12 @@
             pltpu.VMEM((2, LANES, LANES), F32),
             pltpu.VMEM((ROWS, GAUSS), F32),
             pltpu.SemaphoreType.DMA,
+            pltpu.SemaphoreType.DMA,
             pltpu.SemaphoreType.DMA((2 * CHUNKS,)),
         ],
         compiler_params=PARAMS,
         name="scatter",
-    )(returned, basis, jnp.transpose(sends_cur[0]))
+    )(returned, basis, jnp.transpose(sends_cur[0]), image)
     return jnp.transpose(image, (1, 0, 2)), grads
 
 

time: 60.2 us -> 58.8 us (0.977)
  Pallas kernels: 58.7 us -> 57.8 us
  local copies, waits for them, and re-layouts: 0.63 us -> 0 us
    pallas_call x1, Pallas kernels: 48.6 us -> 47.7 us  [body(): pl.pallas_call(main_kernel, out_shape=(shape((3, 16, 256)), shape((384, L...]
    unnamed x3 -> x0, local copies, waits for them, and re-layouts: 0.63 us -> none
where the time goes in v4:
time: 58.8 us; the launch traced here: 58.6 us
  Pallas kernels  57.8 us (98%)
  between operations  0.8 us (1%)
    pallas_call x1, Pallas kernels, body(): pl.pallas_call(main_kernel, out_shape=(shape((3, 16, 256)), shape((384, L...  47.7 us
    pallas_call x1, Pallas kernels, body(): pl.pallas_call(scatter_kernel, out_shape=(shape((ROWS, GAUSS)), shape((3,...  10.1 us

profile of v4, /device:TPU:1, one launch (start us, length us, event | category | flops | bytes accessed | tf_op | source)
XLA Modules:
  0.0 58.6 jit_solution(2445619786402331265)
XLA Ops:
  0.6 47.7 %main.1 = (f32[3,16,256]{2,1,0:T(8,128)}, f32[384,128]{1,0:T(8,128)}, f32[544,128]{1,0:T(8,128)}) custom-call(f32[54,16384]{1,0:T(8,128)} %params.1, s32[16,256]{1,0:T(8,128)} %lists_next.1, s32[16,256]{1,0:T(8,128)} %lists_cur.1, f32[2,16]{1,0:T(2,128)} %bitcast.14, f32[2,16]{1,0:T(2,128)} %bitcast.15, s32[16]{0:T(128)} %counts_next.1, s32[16]{0:T(128)} %counts_cur.1, ...), custom_call_target="tpu_custom_call" | custom-call | tf_op jit(solution)/shard_map/main/pallas_call | solution.py:650
  48.4 10.1 %scatter.1 = (f32[54,16384]{1,0:T(8,128)}, f32[3,16,256]{2,1,0:T(8,128)}) custom-call(f32[384,128]{1,0:T(8,128)} %get-tuple-element.7.turned, f32[544,128]{1,0:T(8,128)} %get-tuple-element.8.basis, s32[32,128]{1,0:T(8,128)} %bitcast.11, f32[3,16,256]{2,1,0:T(8,128)} %get-tuple-element.9.drawn), custom_call_target="tpu_custom_call" | custom-call | tf_op jit(solution)/shard_map/scatter/pallas_call | solution.py:702
